TPU v7x, 512 devices: a whole 4x4x16 slice. The times are simulated.
512 devices in a mesh: ctx: 16 (over z), tp: 16 (over x, y), dp: 2 (over core).
Axes of the slice: x: 4, y: 4, z: 16, core: 2. Of those that a mesh axis runs over, the one named last changes fastest.
Arguments:
- queries: bfloat16 [4096, 4096], P(('dp', 'ctx'), 'tp'), parts along dimension 0, may hold values from -6 to 6
- keys: bfloat16 [4096, 4096], P(('dp', 'ctx'), 'tp'), parts along dimension 0, may hold values from -6 to 6
- values: bfloat16 [4096, 4096], P(('dp', 'ctx'), 'tp'), parts along dimension 0, may hold values from -6 to 6
- residues: float32 [4096, 16], P('tp'), may hold values from -1.5 to 1.5
- decays: float32 [4096, 16], P('tp'), as said below
- skip: float32 [4096], P('tp'), may hold values from -0.5 to 0.5
- out_weight: bfloat16 [4096, 4096], P('tp'), may hold values from -0.09375 to 0.09375
Outputs:
- projected: bfloat16 [4096, 4096], P(('dp', 'ctx', 'tp')), parts along dimension 0
There are 2 independent parts, one for each index of `dp`. A program takes and returns all parts, laid end to end along the dimension named above; an argument that names none is the same for every part. Nothing has to cross between parts.
Inputs may be any that keep to these rules, and one draw needn't show every extreme that they name: `decays`: decay rates are at least 1 / 8192.
All inputs are finite; a program needn't handle non-finite values.
Results may differ from a plain program's by a relative error of at most 0.023.
Values may be sent and summed in bfloat16 or wider, within the bound.
A program may use at most 64 MiB of HBM per device.

v0:
```python
import math

import jax
import jax.numpy as jnp
from jax import lax
from jax.sharding import PartitionSpec as P

precise = lax.Precision.HIGHEST


def swapped(block, axis, distance):
    count = lax.axis_size(axis)
    route = []
    for low in range(count):
        high = low | 1 << distance
        if high != low and high < count:
            route += [(low, high), (high, low)]
    return lax.ppermute(block, axis, route)


def angle_table(row_count, col_count, period):
    product = (
        jnp.arange(row_count, dtype=jnp.int32)[:, None]
        * jnp.arange(col_count, dtype=jnp.int32)[None, :]
        % period
    )
    angles = product.astype(jnp.float32) * (2.0 * math.pi / period)
    return (jnp.cos(angles), jnp.sin(angles))


def transform(table_cos, table_sin, re_part, im_part, forward):
    cos_re = jnp.einsum("kn,rnc->rkc", table_cos, re_part, precision=precise)
    cos_im = jnp.einsum("kn,rnc->rkc", table_cos, im_part, precision=precise)
    sin_re = jnp.einsum("kn,rnc->rkc", table_sin, re_part, precision=precise)
    sin_im = jnp.einsum("kn,rnc->rkc", table_sin, im_part, precision=precise)
    if forward:
        return (cos_re + sin_im, cos_im - sin_re)
    return (cos_re - sin_im, cos_im + sin_re)


def filter_spectrum(residues, decays, fine_freq, length, seq_total):
    half_angle = fine_freq.astype(jnp.float32) * (math.pi / length)
    phase_sin = jnp.sin(2.0 * half_angle)
    half_square = jnp.sin(half_angle) ** 2
    parity_sign = 1.0 - 2.0 * (fine_freq % 2).astype(jnp.float32)

    def add_mode(mode_index, running):
        filter_re, filter_im = running
        decay_rate = lax.dynamic_index_in_dim(decays, mode_index, 1, keepdims=False)
        weight = lax.dynamic_index_in_dim(residues, mode_index, 1, keepdims=False)
        forget = -jnp.expm1(-decay_rate)
        retain = jnp.exp(-decay_rate)
        amplitude = (
            weight
            * jnp.sqrt(2.0 * decay_rate)
            * (1.0 - parity_sign * jnp.exp(-decay_rate * float(seq_total)))
        )
        magnitude = forget * forget + 4.0 * retain * half_square
        filter_re = filter_re + amplitude * (forget + 2.0 * retain * half_square) / magnitude
        filter_im = filter_im - amplitude * retain * phase_sin / magnitude
        return (filter_re, filter_im)

    zero_fill = jnp.zeros((2, fine_freq.shape[1], residues.shape[0]), jnp.float32)
    return lax.fori_loop(0, residues.shape[1], add_mode, (zero_fill, zero_fill))


def forward_section(spectral, ctx_index, bit_number):
    half_span = 1 << bit_number
    partner = swapped(spectral.astype(jnp.bfloat16), "ctx", bit_number).astype(spectral.dtype)
    upper_side = jnp.bitwise_and(jnp.right_shift(ctx_index, bit_number), 1) == 1
    position = jnp.bitwise_and(ctx_index, half_span - 1).astype(jnp.float32)
    angles = position * (math.pi / half_span)
    cosine = jnp.cos(angles)
    sine_part = jnp.sin(angles)
    summed = spectral + partner
    difference = partner - spectral
    rotated = jnp.stack(
        [
            difference[0] * cosine + difference[1] * sine_part,
            difference[1] * cosine - difference[0] * sine_part,
        ]
    )
    return jnp.where(upper_side, rotated, summed)


def inverse_section(spectral, ctx_index, bit_number):
    half_span = 1 << bit_number
    partner = swapped(spectral.astype(jnp.bfloat16), "ctx", bit_number).astype(spectral.dtype)
    upper_side = jnp.bitwise_and(jnp.right_shift(ctx_index, bit_number), 1) == 1
    position = jnp.bitwise_and(ctx_index, half_span - 1).astype(jnp.float32)
    angles = position * (math.pi / half_span)
    cosine = jnp.cos(angles)
    sine_part = jnp.sin(angles)

    def turned(vector):
        return jnp.stack(
            [vector[0] * cosine - vector[1] * sine_part, vector[1] * cosine + vector[0] * sine_part]
        )

    lower_val = spectral + turned(partner)
    upper_val = partner - turned(spectral)
    return jnp.where(upper_side, upper_val, lower_val)


def bit_reverse(ctx_index, bit_count):
    reversed_index = jnp.zeros((), jnp.int32)
    for bit_number in range(bit_count):
        taken = jnp.bitwise_and(jnp.right_shift(ctx_index, bit_number), 1)
        reversed_index = reversed_index + jnp.left_shift(taken, bit_count - 1 - bit_number)
    return reversed_index


def on_device(queries, keys, values, residues, decays, skip, out_weight):
    tokens, channels = keys.shape
    ctx_count = lax.axis_size("ctx")
    ctx_index = lax.axis_index("ctx")
    seq_total = tokens * ctx_count
    length = 2 * seq_total
    key_value = keys.astype(jnp.float32) * values.astype(jnp.float32)
    bit_count = ctx_count.bit_length() - 1
    phase_shift = ctx_index.astype(jnp.float32) * (math.pi / ctx_count)
    zero_fill = jnp.zeros_like(key_value)
    spectral = jnp.stack(
        [
            jnp.stack([key_value, key_value * jnp.cos(phase_shift)]),
            jnp.stack([zero_fill, -key_value * jnp.sin(phase_shift)]),
        ]
    )
    for bit_number in reversed(range(bit_count)):
        spectral = forward_section(spectral, ctx_index, bit_number)
    freq_slot = bit_reverse(ctx_index, bit_count)
    coarse_freq = 2 * freq_slot + jnp.arange(2, dtype=jnp.int32)[:, None]
    token_pos = jnp.arange(tokens, dtype=jnp.int32)[None, :]
    twiddle = (token_pos * coarse_freq % length).astype(jnp.float32) * (2.0 * math.pi / length)
    twiddle_cos = jnp.cos(twiddle)[:, :, None]
    twiddle_sin = jnp.sin(twiddle)[:, :, None]
    re_part = spectral[0] * twiddle_cos + spectral[1] * twiddle_sin
    im_part = spectral[1] * twiddle_cos - spectral[0] * twiddle_sin
    local_cos, local_sin = angle_table(tokens, tokens, tokens)
    re_part, im_part = transform(local_cos, local_sin, re_part, im_part, True)
    fine_freq = (coarse_freq + 2 * ctx_count * token_pos)[:, :, None]
    filter_re, filter_im = filter_spectrum(residues, decays, fine_freq, length, seq_total)
    re_part, im_part = (
        re_part * filter_re - im_part * filter_im,
        re_part * filter_im + im_part * filter_re,
    )
    re_part, im_part = transform(local_cos, local_sin, re_part, im_part, False)
    spectrum_back = jnp.stack(
        [
            re_part * twiddle_cos - im_part * twiddle_sin,
            im_part * twiddle_cos + re_part * twiddle_sin,
        ]
    )
    for bit_number in range(bit_count):
        spectrum_back = inverse_section(spectrum_back, ctx_index, bit_number)
    convolved = (
        spectrum_back[0, 0]
        + spectrum_back[0, 1] * jnp.cos(phase_shift)
        - spectrum_back[1, 1] * jnp.sin(phase_shift)
    ) / float(length)
    gated_rows = (queries.astype(jnp.float32) * (convolved + skip[None, :] * key_value)).astype(
        jnp.bfloat16
    )
    return lax.psum_scatter(
        jnp.dot(gated_rows, out_weight, preferred_element_type=jnp.float32).astype(jnp.bfloat16),
        "tp",
        scatter_dimension=0,
        tiled=True,
    )


def solution(mesh):
    placed = (
        P(("dp", "ctx"), "tp"),
        P(("dp", "ctx"), "tp"),
        P(("dp", "ctx"), "tp"),
        P("tp", None),
        P("tp", None),
        P("tp"),
        P("tp", None),
    )
    return jax.shard_map(
        on_device,
        mesh=mesh,
        in_specs=placed,
        out_specs=P(("dp", "ctx", "tp"), None),
        check_vma=False,
    )
```

profile of v0, /device:TPU:32, one launch (start us, length us, event | category | flops | bytes accessed | tf_op | source)
XLA Modules:
  0.0 376.9 jit_solution(12533975823856944834)
XLA Ops:
  8.9 14.8 %collective-permute-start = (bf16[2,2,128,256]{2,3,1,0:T(8,128)(2,1)S(1)}, bf16[2,2,128,256]{2,3,1,0:T(8,128)(2,1)S(1)}, u32[]{:S(2)}, u32[]{:S(2)}) collective-permute-start(bf16[2,2,128,256]{2,3,1,0:T(8,128)(2,1)S(1)} %fusion.31), channel_id=1, source_target_pairs={{0,256},{256,0},{32,288},{288,32},{64,320},{320,64},{96,352},{352,... | collective-permute-start | bytes 786440 | tf_op jit(solution)/shard_map/ppermute | solution.py:18
  23.9 23.2 %collective-permute-done = bf16[2,2,128,256]{2,3,1,0:T(8,128)(2,1)S(1)} collective-permute-done((bf16[2,2,128,256]{2,3,1,0:T(8,128)(2,1)S(1)}, bf16[2,2,128,256]{2,3,1,0:T(8,128)(2,1)S(1)}, u32[]{:S(2)}, u32[]{:S(2)}) %collective-permute-start) | collective-permute-done | bytes 262176 | tf_op jit(solution)/shard_map/ppermute | solution.py:18
  48.0 1.9 collective-permute-start.1
  50.0 16.9 %collective-permute-done.1 = bf16[2,2,128,256]{2,3,1,0:T(8,128)(2,1)S(1)} collective-permute-done((bf16[2,2,128,256]{2,3,1,0:T(8,128)(2,1)}, bf16[2,2,128,256]{2,3,1,0:T(8,128)(2,1)S(1)}, u32[]{:S(2)}, u32[]{:S(2)}) %collective-permute-start.1) | collective-permute-done | bytes 262176 | tf_op jit(solution)/shard_map/ppermute | solution.py:18
  67.9 5.0 %collective-permute-start.2 = (bf16[2,2,128,256]{2,3,1,0:T(8,128)(2,1)}, bf16[2,2,128,256]{2,3,1,0:T(8,128)(2,1)S(1)}, u32[]{:S(2)}, u32[]{:S(2)}) collective-permute-start(bf16[2,2,128,256]{2,3,1,0:T(8,128)(2,1)} %get-tuple-element.261), channel_id=1, source_target_pairs={{0,64},{64,0},{32,96},{96,32},{128,192},{192,128},{160,224},{224,1... | collective-permute-start | bytes 786440 | tf_op jit(solution)/shard_map/ppermute | solution.py:18
  74.1 8.6 %collective-permute-done.2 = bf16[2,2,128,256]{2,3,1,0:T(8,128)(2,1)S(1)} collective-permute-done((bf16[2,2,128,256]{2,3,1,0:T(8,128)(2,1)}, bf16[2,2,128,256]{2,3,1,0:T(8,128)(2,1)S(1)}, u32[]{:S(2)}, u32[]{:S(2)}) %collective-permute-start.2) | collective-permute-done | bytes 262176 | tf_op jit(solution)/shard_map/ppermute | solution.py:18
  83.7 5.1 %collective-permute-start.3 = (bf16[2,2,128,256]{2,3,1,0:T(8,128)(2,1)}, bf16[2,2,128,256]{2,3,1,0:T(8,128)(2,1)S(1)}, u32[]{:S(2)}, u32[]{:S(2)}) collective-permute-start(bf16[2,2,128,256]{2,3,1,0:T(8,128)(2,1)} %get-tuple-element.259), channel_id=1, source_target_pairs={{0,32},{32,0},{64,96},{96,64},{128,160},{160,128},{192,224},{224,1... | collective-permute-start | bytes 786440 | tf_op jit(solution)/shard_map/ppermute | solution.py:18
  88.9 66.5 %while.18 = (s32[]{:T(128)}, f32[2,128,256]{2,1,0:T(8,128)S(1)}, f32[2,128,256]{2,1,0:T(8,128)S(1)}, f32[256,16]{0,1:T(8,128)}, f32[256,16]{0,1:T(8,128)}, /*ind...) while((s32[]{:T(128)}, f32[2,128,256]{2,1,0:T(8,128)S(1)}, ...), condition=%wide.region_1.2_spmd.clone.clone.clone, body=%wide.region_0.1_spmd.clone.clone.clone.sunk | while | flops 1055491 | bytes 1072755 | solution.py:64
  88.9 1.4 sqrt_multiply_fusion.2
  90.8 1.3 fusion.134
  95.0 1.3 fusion.134
  99.2 1.3 fusion.134
  103.3 1.3 fusion.134
  107.5 1.3 fusion.134
  111.6 1.3 fusion.134
  115.8 1.3 fusion.134
  119.9 1.3 fusion.134
  124.1 1.3 fusion.134
  128.2 1.3 fusion.134
  132.4 1.3 fusion.134
  136.5 1.3 fusion.134
  163.2 1.9 collective-permute-start.4
  165.1 7.9 %collective-permute-done.4 = bf16[2,2,128,256]{2,3,1,0:T(8,128)(2,1)S(1)} collective-permute-done((bf16[2,2,128,256]{2,3,1,0:T(8,128)(2,1)S(1)}, bf16[2,2,128,256]{2,3,1,0:T(8,128)(2,1)S(1)}, u32[]{:S(2)}, u32[]{:S(2)}) %collective-permute-start.4) | collective-permute-done | bytes 262176 | tf_op jit(solution)/shard_map/ppermute | solution.py:18
  173.2 1.9 collective-permute-start.5
  175.2 10.4 %collective-permute-done.5 = bf16[2,2,128,256]{2,3,1,0:T(8,128)(2,1)S(1)} collective-permute-done((bf16[2,2,128,256]{2,3,1,0:T(8,128)(2,1)S(1)}, bf16[2,2,128,256]{2,3,1,0:T(8,128)(2,1)S(1)}, u32[]{:S(2)}, u32[]{:S(2)}) %collective-permute-start.5) | collective-permute-done | bytes 262176 | tf_op jit(solution)/shard_map/ppermute | solution.py:18
  185.8 1.9 collective-permute-start.6
  187.8 23.3 %collective-permute-done.6 = bf16[2,2,128,256]{2,3,1,0:T(8,128)(2,1)S(1)} collective-permute-done((bf16[2,2,128,256]{2,3,1,0:T(8,128)(2,1)S(1)}, bf16[2,2,128,256]{2,3,1,0:T(8,128)(2,1)S(1)}, u32[]{:S(2)}, u32[]{:S(2)}) %collective-permute-start.6) | collective-permute-done | bytes 262176 | tf_op jit(solution)/shard_map/ppermute | solution.py:18
  211.4 12.6 %collective-permute-start.7 = (bf16[2,2,128,256]{2,3,1,0:T(8,128)(2,1)S(1)}, bf16[2,2,128,256]{2,3,1,0:T(8,128)(2,1)S(1)}, u32[]{:S(2)}, u32[]{:S(2)}) collective-permute-start(bf16[2,2,128,256]{2,3,1,0:T(8,128)(2,1)S(1)} %get-tuple-element.250), channel_id=1, source_target_pairs={{0,256},{256,0},{32,288},{288,32},{64,320},{320,64},{96,352},{352,... | collective-permute-start | bytes 786440 | tf_op jit(solution)/shard_map/ppermute | solution.py:18
  224.2 18.7 %collective-permute-done.7 = bf16[2,2,128,256]{2,3,1,0:T(8,128)(2,1)S(1)} collective-permute-done((bf16[2,2,128,256]{2,3,1,0:T(8,128)(2,1)S(1)}, bf16[2,2,128,256]{2,3,1,0:T(8,128)(2,1)S(1)}, u32[]{:S(2)}, u32[]{:S(2)}) %collective-permute-start.7) | collective-permute-done | bytes 262176 | tf_op jit(solution)/shard_map/ppermute | solution.py:18
  243.1 1.5 convolution_convert_fusion
  246.6 121.9 %all-reduce.4.cloned.1.call-done = bf16[128,4096]{1,0:T(8,128)(2,1)} async-done(((bf16[128,4096]{1,0:T(8,128)(2,1)}), bf16[128,4096]{1,0:T(8,128)(2,1)}) %all-reduce.4.cloned.1.call-update) | async-done | bytes 1048592
  368.5 1.5 constant_dynamic-slice_fusion.1
  (117 shorter events, 64.8 us)
Async XLA Ops:
  6.5 236.6 %copy-start = (bf16[256,4096]{1,0:T(8,128)(2,1)S(1)}, bf16[256,4096]{1,0:T(8,128)(2,1)}, u32[]{:S(2)}) copy-start(bf16[256,4096]{1,0:T(8,128)(2,1)} %param.15) | copy-start | bytes 6291460
  6.5 362.0 %all-reduce.4.cloned.1.call-start = ((), (), s32[]{:S(2)}) async-start(), calls=%async_computation | async-start | bytes 2097152
  8.9 38.2 %collective-permute-start = (bf16[2,2,128,256]{2,3,1,0:T(8,128)(2,1)S(1)}, bf16[2,2,128,256]{2,3,1,0:T(8,128)(2,1)S(1)}, u32[]{:S(2)}, u32[]{:S(2)}) collective-permute-start(bf16[2,2,128,256]{2,3,1,0:T(8,128)(2,1)S(1)} %fusion.31), channel_id=1, source_target_pairs={{0,256},{256,0},{32,288},{288,32},{64,320},{320,64},{96,352},{352,... | collective-permute-start | bytes 786440 | tf_op jit(solution)/shard_map/ppermute | solution.py:18
  48.0 19.0 %collective-permute-start.1 = (bf16[2,2,128,256]{2,3,1,0:T(8,128)(2,1)}, bf16[2,2,128,256]{2,3,1,0:T(8,128)(2,1)S(1)}, u32[]{:S(2)}, u32[]{:S(2)}) collective-permute-start(bf16[2,2,128,256]{2,3,1,0:T(8,128)(2,1)} %get-tuple-element.263), channel_id=1, source_target_pairs={{0,128},{128,0},{32,160},{160,32},{64,192},{192,64},{96,224},{224,... | collective-permute-start | bytes 786440 | tf_op jit(solution)/shard_map/ppermute | solution.py:18
  67.9 14.8 %collective-permute-start.2 = (bf16[2,2,128,256]{2,3,1,0:T(8,128)(2,1)}, bf16[2,2,128,256]{2,3,1,0:T(8,128)(2,1)S(1)}, u32[]{:S(2)}, u32[]{:S(2)}) collective-permute-start(bf16[2,2,128,256]{2,3,1,0:T(8,128)(2,1)} %get-tuple-element.261), channel_id=1, source_target_pairs={{0,64},{64,0},{32,96},{96,32},{128,192},{192,128},{160,224},{224,1... | collective-permute-start | bytes 786440 | tf_op jit(solution)/shard_map/ppermute | solution.py:18
  83.7 74.1 %collective-permute-start.3 = (bf16[2,2,128,256]{2,3,1,0:T(8,128)(2,1)}, bf16[2,2,128,256]{2,3,1,0:T(8,128)(2,1)S(1)}, u32[]{:S(2)}, u32[]{:S(2)}) collective-permute-start(bf16[2,2,128,256]{2,3,1,0:T(8,128)(2,1)} %get-tuple-element.259), channel_id=1, source_target_pairs={{0,32},{32,0},{64,96},{96,64},{128,160},{160,128},{192,224},{224,1... | collective-permute-start | bytes 786440 | tf_op jit(solution)/shard_map/ppermute | solution.py:18
  88.9 68.9 %copy-start.1 = (f32[2,2,128,256]{2,3,1,0:T(8,128)S(1)}, f32[2,2,128,256]{2,3,1,0:T(8,128)}, u32[]{:S(2)}) copy-start(f32[2,2,128,256]{2,3,1,0:T(8,128)} %get-tuple-element.260) | copy-start | bytes 1572868
  158.0 2.0 copy-start.2
  158.0 2.0 copy-start.3
  163.2 9.9 %collective-permute-start.4 = (bf16[2,2,128,256]{2,3,1,0:T(8,128)(2,1)S(1)}, bf16[2,2,128,256]{2,3,1,0:T(8,128)(2,1)S(1)}, u32[]{:S(2)}, u32[]{:S(2)}) collective-permute-start(bf16[2,2,128,256]{2,3,1,0:T(8,128)(2,1)S(1)} %fusion.30), channel_id=1, source_target_pairs={{0,32},{32,0},{64,96},{96,64},{128,160},{160,128},{192,224},{224,1... | collective-permute-start | bytes 786440 | tf_op jit(solution)/shard_map/ppermute | solution.py:18
  173.2 12.4 %collective-permute-start.5 = (bf16[2,2,128,256]{2,3,1,0:T(8,128)(2,1)S(1)}, bf16[2,2,128,256]{2,3,1,0:T(8,128)(2,1)S(1)}, u32[]{:S(2)}, u32[]{:S(2)}) collective-permute-start(bf16[2,2,128,256]{2,3,1,0:T(8,128)(2,1)S(1)} %get-tuple-element.254), channel_id=1, source_target_pairs={{0,64},{64,0},{32,96},{96,32},{128,192},{192,128},{160,224},{224,1... | collective-permute-start | bytes 786440 | tf_op jit(solution)/shard_map/ppermute | solution.py:18
  185.8 25.3 %collective-permute-start.6 = (bf16[2,2,128,256]{2,3,1,0:T(8,128)(2,1)S(1)}, bf16[2,2,128,256]{2,3,1,0:T(8,128)(2,1)S(1)}, u32[]{:S(2)}, u32[]{:S(2)}) collective-permute-start(bf16[2,2,128,256]{2,3,1,0:T(8,128)(2,1)S(1)} %get-tuple-element.252), channel_id=1, source_target_pairs={{0,128},{128,0},{32,160},{160,32},{64,192},{192,64},{96,224},{224,... | collective-permute-start | bytes 786440 | tf_op jit(solution)/shard_map/ppermute | solution.py:18
  187.8 36.2 %copy-start.4 = (bf16[128,256]{1,0:T(8,128)(2,1)S(1)}, bf16[128,256]{1,0:T(8,128)(2,1)}, u32[]{:S(2)}) copy-start(bf16[128,256]{1,0:T(8,128)(2,1)} %param.9) | copy-start | bytes 196612
  211.4 31.5 %collective-permute-start.7 = (bf16[2,2,128,256]{2,3,1,0:T(8,128)(2,1)S(1)}, bf16[2,2,128,256]{2,3,1,0:T(8,128)(2,1)S(1)}, u32[]{:S(2)}, u32[]{:S(2)}) collective-permute-start(bf16[2,2,128,256]{2,3,1,0:T(8,128)(2,1)S(1)} %get-tuple-element.250), channel_id=1, source_target_pairs={{0,256},{256,0},{32,288},{288,32},{64,320},{320,64},{96,352},{352,... | collective-permute-start | bytes 786440 | tf_op jit(solution)/shard_map/ppermute | solution.py:18
  224.2 18.9 %copy-start.5 = (f32[256]{0:T(256)S(1)}, f32[256]{0:T(256)}, u32[]{:S(2)}) copy-start(f32[256]{0:T(256)} %param.14) | copy-start | bytes 3076
Sparse Core Ops, SparseCore 0:
  244.8 123.7 all-reduce.3
where the time goes:
time: 380 us; the launch traced here: 377 us
  waiting for transfers between devices  231 us (61%)
  other arithmetic  72.1 us (19%)
  starting transfers between devices  45.2 us (12%)
  between operations  15.2 us (4%)
  local copies, waits for them, and re-layouts  6.56 us (2%)
  matrix products  6.53 us (2%)
    unnamed x2, waiting for transfers between devices  122 us
    ppermute x8, waiting for transfers between devices, swapped(): return lax.ppermute(block, axis, route)  109 us
    ppermute x8, starting transfers between devices, swapped(): return lax.ppermute(block, axis, route)  45.2 us
    mul x16, other arithmetic, add_mode(): filter_im = filter_im - amplitude * retain * phase_sin / magnitude  21.4 us
    mul x16, other arithmetic, add_mode(): weight * jnp.sqrt(2.0 * decay_rate)  20.9 us
    sub x16, other arithmetic, add_mode(): filter_im = filter_im - amplitude * retain * phase_sin / magnitude  14.7 us
    mul x16, other arithmetic, add_mode(): 2.0 * retain * half_square  9.07 us
  transfers between devices with their start and end apart: 9, of which 8 were waited for; matrix products, arithmetic and copies ran while one was open for 19% of the time, Pallas kernels for 0%

commit v1 on v0

v1 whole, which is shorter than its diff:
```python
import functools

import jax
import jax.numpy as jnp
from jax import lax
from jax.experimental import pallas as pl
from jax.experimental.pallas import tpu as pltpu
from jax.sharding import PartitionSpec as P

MESH = pl.DeviceIdType.MESH
F32 = jnp.float32
BF16 = jnp.bfloat16

SIDE = 4
SUB = 8
FIRST = (0, 0, 1, 1, 3, 3, 3, 5, 6, 6, 6, 6, 6, 6, 6, 6)
CHUNKS = 2


def pick(table, index):
    value = jnp.int32(table[0])
    for position in range(1, len(table)):
        value = jnp.where(index == position, jnp.int32(table[position]), value)
    return value


def remote(src, dst, send_sem, recv_sem, device):
    return pltpu.make_async_remote_copy(
        src_ref=src,
        dst_ref=dst,
        send_sem=send_sem,
        recv_sem=recv_sem,
        device_id=device,
        device_id_type=MESH,
    )


def operator_kernel(
    q_hbm,
    k_hbm,
    v_hbm,
    res_hbm,
    dec_hbm,
    skip_hbm,
    w_hbm,
    out_ref,
    q_in,
    k_in,
    v_in,
    res,
    dec,
    skip,
    weight,
    xpad,
    kern,
    conv,
    gain,
    step8,
    state,
    carry,
    own_msg,
    pre_msg,
    got,
    gated,
    part,
    part_in,
    half_sum,
    half_in,
    in_sem,
    e_send,
    p_send,
    c_recv,
    r1_send,
    r1_recv,
    r2_send,
    r2_recv,
):
    blocks = len(FIRST)
    tokens, channels = k_in.shape
    groups = tokens // SUB
    modes = res.shape[0]
    width = part.shape[3]
    z = lax.axis_index("ctx")
    tp = lax.axis_index("tp")
    x, y = tp // SIDE, tp % SIDE

    def line(axis, shift):
        if axis == 0:
            return {"tp": (x + shift) % SIDE * SIDE + y}
        return {"tp": x * SIDE + (y + shift) % SIDE}

    first = pick(FIRST, z)
    fan_out = pick(
        [sum(FIRST[j] <= i < j for j in range(blocks)) for i in range(blocks)], z
    )
    sends_prefix = functools.reduce(
        jnp.logical_or, [z == i for i in sorted(set(FIRST[1:]))]
    )

    barrier = pltpu.get_barrier_semaphore()
    for shift in range(1, SIDE):
        for axis in (0, 1):
            pl.semaphore_signal(
                barrier, inc=1, device_id=line(axis, shift), device_id_type=MESH
            )

    @pl.loop(first, z)
    def _(source):
        pl.semaphore_signal(
            barrier, inc=1, device_id={"ctx": source}, device_id_type=MESH
        )

    loads = [
        pltpu.make_async_copy(src, dst, in_sem.at[i])
        for i, (src, dst) in enumerate(
            (
                (k_hbm, k_in),
                (v_hbm, v_in),
                (dec_hbm, dec),
                (res_hbm, res),
                (q_hbm, q_in),
                (skip_hbm, skip),
                (w_hbm, weight),
            )
        )
    ]
    for load in loads:
        load.start()
    for load in loads[:4]:
        load.wait()

    xpad[pl.ds(0, SUB), :] = jnp.zeros((SUB, channels), F32)
    xpad[pl.ds(SUB, tokens), :] = k_in[...].astype(F32) * v_in[...].astype(F32)

    row = lax.broadcasted_iota(jnp.int32, (SUB, channels), 0).astype(F32)
    for s in range(modes):
        rate = jnp.broadcast_to(dec[pl.ds(s, 1), :], (SUB, channels))
        amp = jnp.broadcast_to(res[pl.ds(s, 1), :], (SUB, channels)) * jnp.sqrt(
            2.0 * rate
        )
        a8 = jnp.exp(-float(SUB) * rate)
        step8[s] = a8
        gain[s] = amp * jnp.exp(-rate * row)
        total = xpad[pl.ds(SUB, SUB), :]
        for m in range(1, groups):
            total = total * a8 + xpad[pl.ds(SUB * (m + 1), SUB), :]
        total = total * jnp.exp(rate * (row - float(SUB - 1)))
        state[pl.ds(s, 1), :] = jnp.sum(total, axis=0, keepdims=True)
    own_msg[...] = state[...].astype(BF16)
    decay_block = jnp.exp(-float(tokens) * dec[...])

    pl.semaphore_wait(barrier, 2 * (SIDE - 1) + fan_out)

    for j in range(1, blocks):

        @pl.when(jnp.logical_and(z > FIRST[j], z < j))
        def _():
            remote(
                own_msg, got.at[z], e_send.at[j], c_recv.at[z], {"ctx": jnp.int32(j)}
            ).start()

    def receive_carry():
        carry[...] = jnp.zeros_like(carry)

        @pl.loop(first, z)
        def _(source):
            remote(
                own_msg, got.at[source], e_send.at[0], c_recv.at[source], {"ctx": z}
            ).wait_recv()
            carry[...] = carry[...] * decay_block + got[source].astype(F32)

    @pl.when(sends_prefix)
    def _():
        receive_carry()
        pre_msg[...] = (state[...] + decay_block * carry[...]).astype(BF16)
        for j in range(1, blocks):

            @pl.when(z == FIRST[j])
            def _():
                remote(
                    pre_msg,
                    got.at[z],
                    p_send.at[j],
                    c_recv.at[z],
                    {"ctx": jnp.int32(j)},
                ).start()

    for half in range(2):
        lanes = pl.ds(half * (channels // 2), channels // 2)
        base = [gain[s, :, lanes] for s in range(modes)]
        for m in range(groups):
            kern[pl.ds(SUB * m, SUB), lanes] = sum(base[1:], base[0])
            if m + 1 < groups:
                base = [b * step8[s, :, lanes] for s, b in enumerate(base)]
    loads[5].wait()
    conv[...] = jnp.broadcast_to(skip[...], (tokens, channels)) * xpad[pl.ds(SUB, tokens), :]
    for m in range(groups):
        rows = tokens - SUB * m
        conv[pl.ds(SUB * m, rows), :] += sum(
            jnp.broadcast_to(kern[pl.ds(SUB * m + f, 1), :], (rows, channels))
            * xpad[pl.ds(SUB - f, rows), :]
            for f in range(SUB)
        )
    loads[4].wait()

    @pl.when(jnp.logical_not(sends_prefix))
    def _():
        receive_carry()

    for half in range(2):
        lanes = pl.ds(half * (channels // 2), channels // 2)
        base = []
        for s in range(modes):
            a1 = jnp.exp(-dec[pl.ds(s, 1), lanes])
            base.append(
                gain[s, :, lanes]
                * jnp.broadcast_to(a1 * carry[pl.ds(s, 1), lanes], (SUB, channels // 2))
            )
        for m in range(groups):
            here = pl.ds(SUB * m, SUB)
            conv[here, lanes] += sum(base[1:], base[0])
            if m + 1 < groups:
                base = [b * step8[s, :, lanes] for s, b in enumerate(base)]
    product = q_in[...].astype(F32) * conv[...]
    gated[0] = product.astype(BF16)
    gated[1] = jnp.concatenate(
        [
            product[SUB * (SIDE * i + j) : SUB * (SIDE * i + j + 1)]
            for j in range(SIDE)
            for i in range(SIDE)
        ],
        axis=0,
    ).astype(BF16)

    loads[6].wait()
    place = (x, y)
    band = SIDE * SUB
    order = (2, 1, 3)

    def first_copy(c, h, shift):
        target = (place[h] + shift) % SIDE
        return remote(
            part.at[c, h, pl.ds(pl.multiple_of(target * band, band), band)],
            part_in.at[c, h, shift - 1],
            r1_send.at[c, h, shift - 1],
            r1_recv.at[c, h, shift - 1],
            line(h, shift),
        )

    def second_copy(c, h, shift):
        target = (place[1 - h] + shift) % SIDE
        return remote(
            half_sum.at[c, h, target],
            half_in.at[c, h, shift - 1],
            r2_send.at[c, h, shift - 1],
            r2_recv.at[c, h, shift - 1],
            line(1 - h, shift),
        )

    for c in range(CHUNKS):
        for h in range(2):
            columns = pl.ds((h * CHUNKS + c) * width, width)
            part[c, h] = jnp.dot(
                gated[h], weight[:, columns], preferred_element_type=F32
            ).astype(BF16)
            for shift in order:
                first_copy(c, h, shift).start()

    for c in range(CHUNKS):
        for h in range(2):
            mine = pl.ds(pl.multiple_of(place[h] * band, band), band)
            total = part[c, h, mine].astype(F32)
            for shift in order:
                first_copy(c, h, shift).wait_recv()
                total = total + part_in[c, h, shift - 1].astype(F32)
            for i in range(SIDE):
                rows = total[SUB * i : SUB * (i + 1)]
                half_sum[c, h, i] = jnp.concatenate(
                    [rows[:, : width // 2], rows[:, width // 2 :]], axis=0
                ).astype(BF16)
            for shift in order:
                second_copy(c, h, shift).start()

    for c in range(CHUNKS):
        for h in range(2):
            total = half_sum[c, h, place[1 - h]].astype(F32)
            for shift in order:
                second_copy(c, h, shift).wait_recv()
                total = total + half_in[c, h, shift - 1].astype(F32)
            start = (h * CHUNKS + c) * width
            out_ref[:, pl.ds(start, width // 2)] = total[:SUB].astype(BF16)
            out_ref[:, pl.ds(start + width // 2, width // 2)] = total[SUB:].astype(BF16)

    for c in range(CHUNKS):
        for h in range(2):
            for shift in order:
                first_copy(c, h, shift).wait_send()
                second_copy(c, h, shift).wait_send()
    for j in range(1, blocks):

        @pl.when(jnp.logical_and(z > FIRST[j], z < j))
        def _():
            remote(
                own_msg, got.at[z], e_send.at[j], c_recv.at[z], {"ctx": jnp.int32(j)}
            ).wait_send()

        @pl.when(z == FIRST[j])
        def _():
            remote(
                pre_msg, got.at[z], p_send.at[j], c_recv.at[z], {"ctx": jnp.int32(j)}
            ).wait_send()


def on_device(queries, keys, values, residues, decays, skip, out_weight):
    tokens, channels = keys.shape
    modes = residues.shape[1]
    features = out_weight.shape[1]
    blocks = len(FIRST)
    width = features // (2 * CHUNKS)
    band = SIDE * SUB
    hbm = pl.BlockSpec(memory_space=pltpu.HBM)
    dma = pltpu.SemaphoreType.DMA
    return pl.pallas_call(
        operator_kernel,
        out_shape=jax.ShapeDtypeStruct((SUB, features), BF16),
        in_specs=[hbm] * 7,
        out_specs=pl.BlockSpec(memory_space=pltpu.VMEM),
        scratch_shapes=[
            pltpu.VMEM((tokens, channels), BF16),
            pltpu.VMEM((tokens, channels), BF16),
            pltpu.VMEM((tokens, channels), BF16),
            pltpu.VMEM((modes, channels), F32),
            pltpu.VMEM((modes, channels), F32),
            pltpu.VMEM((1, channels), F32),
            pltpu.VMEM((channels, features), BF16),
            pltpu.VMEM((tokens + SUB, channels), F32),
            pltpu.VMEM((tokens, channels), F32),
            pltpu.VMEM((tokens, channels), F32),
            pltpu.VMEM((modes, SUB, channels), F32),
            pltpu.VMEM((modes, SUB, channels), F32),
            pltpu.VMEM((modes, channels), F32),
            pltpu.VMEM((modes, channels), F32),
            pltpu.VMEM((modes, channels), BF16),
            pltpu.VMEM((modes, channels), BF16),
            pltpu.VMEM((blocks, modes, channels), BF16),
            pltpu.VMEM((2, tokens, channels), BF16),
            pltpu.VMEM((CHUNKS, 2, tokens, width), BF16),
            pltpu.VMEM((CHUNKS, 2, SIDE - 1, band, width), BF16),
            pltpu.VMEM((CHUNKS, 2, SIDE, 2 * SUB, width // 2), BF16),
            pltpu.VMEM((CHUNKS, 2, SIDE - 1, 2 * SUB, width // 2), BF16),
            dma((7,)),
            dma((blocks,)),
            dma((blocks,)),
            dma((blocks,)),
            dma((CHUNKS, 2, SIDE - 1)),
            dma((CHUNKS, 2, SIDE - 1)),
            dma((CHUNKS, 2, SIDE - 1)),
            dma((CHUNKS, 2, SIDE - 1)),
        ],
        compiler_params=pltpu.CompilerParams(
            collective_id=0, has_side_effects=True, vmem_limit_bytes=48 << 20
        ),
    )(
        queries,
        keys,
        values,
        residues.T,
        decays.T,
        skip.reshape(1, channels),
        out_weight,
    )


def solution(mesh):
    placed = (
        P(("dp", "ctx"), "tp"),
        P(("dp", "ctx"), "tp"),
        P(("dp", "ctx"), "tp"),
        P("tp", None),
        P("tp", None),
        P("tp"),
        P("tp", None),
    )
    return jax.shard_map(
        on_device,
        mesh=mesh,
        in_specs=placed,
        out_specs=P(("dp", "ctx", "tp"), None),
        check_vma=False,
    )
```

time: 380 us -> 36.5 us (0.10)
  the two profiles are of different devices: /device:TPU:32 before, /device:TPU:448 now
where the time goes in v1:
time: 36.5 us; the launch traced here: 36.1 us
  Pallas kernels  29.2 us (80%)
  local copies, waits for them, and re-layouts  6.85 us (19%)
    pallas_call x1, Pallas kernels, on_device(): pl.pallas_call(operator_kernel, out_shape=jax.ShapeDtypeStruct((SUB, feat...  29.2 us
    unnamed x15, local copies, waits for them, and re-layouts  6.85 us

profile of v1, /device:TPU:448, one launch (start us, length us, event | category | flops | bytes accessed | tf_op | source)
XLA Modules:
  0.0 36.1 jit_solution(4183422525446766893)
XLA Ops:
  0.0 0.0 copy-start
  0.0 1.6 %copy-done = bf16[256,4096]{1,0:T(8,128)(2,1)S(1)} copy-done((bf16[256,4096]{1,0:T(8,128)(2,1)S(1)}, bf16[256,4096]{1,0:T(8,128)(2,1)}, u32[]{:S(2)}) %copy-start) | copy-done | bytes 2097176
  1.6 0.0 copy-start.1
  1.6 0.8 %copy-done.1 = bf16[128,256]{1,0:T(8,128)(2,1)S(1)} copy-done((bf16[128,256]{1,0:T(8,128)(2,1)S(1)}, bf16[128,256]{1,0:T(8,128)(2,1)}, u32[]{:S(2)}) %copy-start.1) | copy-done | bytes 65560
  2.4 0.0 copy-start.2
  2.4 0.8 %copy-done.2 = bf16[128,256]{1,0:T(8,128)(2,1)S(1)} copy-done((bf16[128,256]{1,0:T(8,128)(2,1)S(1)}, bf16[128,256]{1,0:T(8,128)(2,1)}, u32[]{:S(2)}) %copy-start.2) | copy-done | bytes 65560
  3.3 0.0 copy-start.3
  3.3 0.8 %copy-done.3 = bf16[128,256]{1,0:T(8,128)(2,1)S(1)} copy-done((bf16[128,256]{1,0:T(8,128)(2,1)S(1)}, bf16[128,256]{1,0:T(8,128)(2,1)}, u32[]{:S(2)}) %copy-start.3) | copy-done | bytes 65560
  4.1 0.0 copy-start.4
  4.1 0.7 %copy-done.4 = f32[256,16]{0,1:T(8,128)S(1)} copy-done((f32[256,16]{0,1:T(8,128)S(1)}, f32[256,16]{0,1:T(8,128)}, u32[]{:S(2)}) %copy-start.4) | copy-done | bytes 16408
  4.8 0.0 copy-start.5
  4.8 0.7 %copy-done.5 = f32[256,16]{0,1:T(8,128)S(1)} copy-done((f32[256,16]{0,1:T(8,128)S(1)}, f32[256,16]{0,1:T(8,128)}, u32[]{:S(2)}) %copy-start.5) | copy-done | bytes 16408
  5.5 0.0 copy-start.6
  5.5 0.7 %copy-done.6 = f32[256]{0:T(256)S(1)} copy-done((f32[256]{0:T(256)S(1)}, f32[256]{0:T(256)}, u32[]{:S(2)}) %copy-start.6) | copy-done | bytes 1048
  6.2 29.2 %shard_map.73 = bf16[8,4096]{1,0:T(8,128)(2,1)S(1)} custom-call(bf16[128,256]{1,0:T(8,128)(2,1)S(1)} %copy-done.1, bf16[128,256]{1,0:T(8,128)(2,1)S(1)} %copy-done.2, bf16[128,256]{1,0:T(8,128)(2,1)S(1)} %copy-done.3, f32[16,256]{1,0:T(8,128)S(1)} %bitcast.3, f32[16,256]{1,0:T(8,128)S(1)} %bitcast.4, f32[1,256]{1,0:T(1,128)S(1)} %bitcast.5, ...), custom_call_target="tpu_custom_call" | custom-call | tf_op jit(solution)/shard_map/pallas_call | solution.py:323
  35.5 0.6 %copy.9 = bf16[8,4096]{1,0:T(8,128)(2,1)} copy(bf16[8,4096]{1,0:T(8,128)(2,1)S(1)} %shard_map.73) | data formatting | bytes 131072
Async XLA Ops:
  0.0 1.6 %copy-start = (bf16[256,4096]{1,0:T(8,128)(2,1)S(1)}, bf16[256,4096]{1,0:T(8,128)(2,1)}, u32[]{:S(2)}) copy-start(bf16[256,4096]{1,0:T(8,128)(2,1)} %w_hbm.1) | copy-start | bytes 6291460
  1.6 0.8 %copy-start.1 = (bf16[128,256]{1,0:T(8,128)(2,1)S(1)}, bf16[128,256]{1,0:T(8,128)(2,1)}, u32[]{:S(2)}) copy-start(bf16[128,256]{1,0:T(8,128)(2,1)} %q_hbm.1) | copy-start | bytes 196612
  2.4 0.8 %copy-start.2 = (bf16[128,256]{1,0:T(8,128)(2,1)S(1)}, bf16[128,256]{1,0:T(8,128)(2,1)}, u32[]{:S(2)}) copy-start(bf16[128,256]{1,0:T(8,128)(2,1)} %k_hbm.1) | copy-start | bytes 196612
  3.3 0.8 %copy-start.3 = (bf16[128,256]{1,0:T(8,128)(2,1)S(1)}, bf16[128,256]{1,0:T(8,128)(2,1)}, u32[]{:S(2)}) copy-start(bf16[128,256]{1,0:T(8,128)(2,1)} %v_hbm.1) | copy-start | bytes 196612
  4.1 0.7 %copy-start.4 = (f32[256,16]{0,1:T(8,128)S(1)}, f32[256,16]{0,1:T(8,128)}, u32[]{:S(2)}) copy-start(f32[256,16]{0,1:T(8,128)} %param.10) | copy-start | bytes 49156
  4.8 0.7 %copy-start.5 = (f32[256,16]{0,1:T(8,128)S(1)}, f32[256,16]{0,1:T(8,128)}, u32[]{:S(2)}) copy-start(f32[256,16]{0,1:T(8,128)} %param.11) | copy-start | bytes 49156
  5.5 0.7 %copy-start.6 = (f32[256]{0:T(256)S(1)}, f32[256]{0:T(256)}, u32[]{:S(2)}) copy-start(f32[256]{0:T(256)} %param.12) | copy-start | bytes 3076

commit v2 on v1

--- a/solution.py
+++ b/solution.py
@@ -322,7 +322,7 @@
     dma = pltpu.SemaphoreType.DMA
     return pl.pallas_call(
         operator_kernel,
-        out_shape=jax.ShapeDtypeStruct((SUB, features), BF16),
+        out_shape=pltpu.VMEM((SUB, features), BF16),
         in_specs=[hbm] * 7,
         out_specs=pl.BlockSpec(memory_space=pltpu.VMEM),
         scratch_shapes=[
@@ -358,7 +358,7 @@
             dma((CHUNKS, 2, SIDE - 1)),
         ],
         compiler_params=pltpu.CompilerParams(
-            collective_id=0, has_side_effects=True, vmem_limit_bytes=48 << 20
+            collective_id=0, has_side_effects=True, vmem_limit_bytes=60 << 20
         ),
     )(
         queries,

time: 36.5 us -> 30 us (0.82)
  local copies, waits for them, and re-layouts: 6.85 us -> 0.63 us
    unnamed x15 -> x1, local copies, waits for them, and re-layouts: 6.85 us -> 0.63 us
where the time goes in v2:
time: 30 us; the launch traced here: 29.9 us
  Pallas kernels  29.2 us (97%)
  local copies, waits for them, and re-layouts  0.63 us (2%)
    pallas_call x1, Pallas kernels, on_device(): pl.pallas_call(operator_kernel, out_shape=pltpu.VMEM((SUB, features), BF1...  29.2 us
    unnamed x1, local copies, waits for them, and re-layouts  0.63 us

profile of v2, /device:TPU:448, one launch (start us, length us, event | category | flops | bytes accessed | tf_op | source)
XLA Modules:
  0.0 29.9 jit_solution(13800139101507357842)
XLA Ops:
  0.0 29.2 %shard_map.73 = bf16[8,4096]{1,0:T(8,128)(2,1)S(1)} custom-call(bf16[128,256]{1,0:T(8,128)(2,1)} %q_hbm.1, bf16[128,256]{1,0:T(8,128)(2,1)} %k_hbm.1, bf16[128,256]{1,0:T(8,128)(2,1)} %v_hbm.1, f32[16,256]{1,0:T(8,128)} %bitcast.3, f32[16,256]{1,0:T(8,128)} %bitcast.4, f32[1,256]{1,0:T(1,128)} %bitcast.5, bf16[256,4096]{1,0:T(8,128)(2,1)} %w_hbm.1), custom_call_target="tpu_custom_call" | custom-call | tf_op jit(solution)/shard_map/pallas_call | solution.py:323
  29.3 0.6 %copy.9 = bf16[8,4096]{1,0:T(8,128)(2,1)} copy(bf16[8,4096]{1,0:T(8,128)(2,1)S(1)} %shard_map.73) | data formatting | bytes 131072

commit v3 on v2

--- a/solution.py
+++ b/solution.py
@@ -13,7 +13,10 @@
 
 SIDE = 4
 SUB = 8
-FIRST = (0, 0, 1, 1, 3, 3, 3, 5, 6, 6, 6, 6, 6, 6, 6, 6)
+HEAD = (0, 0, 1, 0, 3, 3, 3, 6, 6, 6, 6, 6, 1, 1, 1, 1)
+HUB, HUB_HEAD, HUB_LAST, HUB_TO = 1, 3, 6, (12, 13, 14, 15)
+PAIR = 8
+LATE = {HUB: HUB_TO, 6: (8, 9, 10, 11)}
 CHUNKS = 2
 
 
@@ -60,28 +63,35 @@
     carry,
     own_msg,
     pre_msg,
+    hub_msg,
     got,
     gated,
     part,
     part_in,
+    relay_in,
+    relay_out,
     half_sum,
     half_in,
     in_sem,
     e_send,
     p_send,
     c_recv,
+    a_send,
+    a_recv,
     r1_send,
     r1_recv,
     r2_send,
     r2_recv,
+    ready,
 ):
-    blocks = len(FIRST)
+    blocks = len(HEAD)
     tokens, channels = k_in.shape
     groups = tokens // SUB
     modes = res.shape[0]
     width = part.shape[3]
     z = lax.axis_index("ctx")
     tp = lax.axis_index("tp")
+    core = lax.axis_index("dp")
     x, y = tp // SIDE, tp % SIDE
 
     def line(axis, shift):
@@ -89,26 +99,64 @@
             return {"tp": (x + shift) % SIDE * SIDE + y}
         return {"tp": x * SIDE + (y + shift) % SIDE}
 
-    first = pick(FIRST, z)
-    fan_out = pick(
-        [sum(FIRST[j] <= i < j for j in range(blocks)) for i in range(blocks)], z
+    plain = {j: [] for j in range(blocks)}
+    whole = {j: [] for j in range(blocks)}
+    for j in range(1, blocks):
+        start = HEAD[j] + 1 if j <= PAIR else PAIR + 1
+        plain[j] += list(range(start, j))
+        if j > PAIR:
+            whole[j].append(PAIR)
+        if j not in HUB_TO:
+            whole[j].append(HEAD[j])
+    plain[HUB] += list(range(HUB_HEAD + 1, HUB_LAST + 1))
+    whole[HUB].append(HUB_HEAD)
+    late = {j: k for k, group in LATE.items() for j in group}
+    greeted = {
+        j: [k for k in plain[j] + whole[j] if late.get(j) != k] for j in range(blocks)
+    }
+    expected = pick(
+        [
+            sum(i in greeted[j] for j in range(blocks)) + (i in late)
+            for i in range(blocks)
+        ],
+        z,
     )
-    sends_prefix = functools.reduce(
-        jnp.logical_or, [z == i for i in sorted(set(FIRST[1:]))]
-    )
-
+
+    def among(members):
+        return functools.reduce(jnp.logical_or, [z == i for i in sorted(members)])
+
+    heads = among({k for j in range(1, blocks) for k in whole[j]} - {PAIR})
     barrier = pltpu.get_barrier_semaphore()
-    for shift in range(1, SIDE):
+
+    for source in range(blocks):
+        if any(source in greeted[j] for j in range(blocks)):
+
+            @pl.when(among([j for j in range(blocks) if source in greeted[j]]))
+            def _():
+                pl.semaphore_signal(
+                    barrier,
+                    inc=1,
+                    device_id={"ctx": jnp.int32(source)},
+                    device_id_type=MESH,
+                )
+
+    for source, group in LATE.items():
+
+        @pl.when(z == source)
+        def _():
+            for j in group:
+                pl.semaphore_signal(
+                    barrier,
+                    inc=1,
+                    device_id={"ctx": jnp.int32(j)},
+                    device_id_type=MESH,
+                )
+
+    for shift in (2, 1, 3):
         for axis in (0, 1):
             pl.semaphore_signal(
                 barrier, inc=1, device_id=line(axis, shift), device_id_type=MESH
             )
-
-    @pl.loop(first, z)
-    def _(source):
-        pl.semaphore_signal(
-            barrier, inc=1, device_id={"ctx": source}, device_id_type=MESH
-        )
 
     loads = [
         pltpu.make_async_copy(src, dst, in_sem.at[i])
@@ -149,41 +197,95 @@
     own_msg[...] = state[...].astype(BF16)
     decay_block = jnp.exp(-float(tokens) * dec[...])
 
-    pl.semaphore_wait(barrier, 2 * (SIDE - 1) + fan_out)
-
-    for j in range(1, blocks):
-
-        @pl.when(jnp.logical_and(z > FIRST[j], z < j))
+    pl.semaphore_wait(barrier, 2 * (SIDE - 1) + expected)
+    for source, group in LATE.items():
+
+        @pl.when(among(group))
         def _():
-            remote(
-                own_msg, got.at[z], e_send.at[j], c_recv.at[z], {"ctx": jnp.int32(j)}
-            ).start()
+            pl.semaphore_signal(
+                ready,
+                inc=1,
+                device_id={"ctx": jnp.int32(source)},
+                device_id_type=MESH,
+            )
+
+    def message(buffer, sems, j):
+        return remote(
+            buffer, got.at[z], sems.at[j], c_recv.at[z], {"ctx": jnp.int32(j)}
+        )
+
+    def arrived(source):
+        remote(
+            own_msg, got.at[source], e_send.at[0], c_recv.at[source], {"ctx": z}
+        ).wait_recv()
+
+    for j in reversed(range(1, blocks)):
+        if plain[j]:
+
+            @pl.when(among(plain[j]))
+            def _():
+                message(own_msg, e_send, j).start()
 
     def receive_carry():
         carry[...] = jnp.zeros_like(carry)
 
-        @pl.loop(first, z)
+        @pl.when(z > 0)
+        def _():
+            head = pick(HEAD, z)
+            arrived(head)
+            carry[...] = got[head].astype(F32)
+
+        @pl.when(z > PAIR)
+        def _():
+            arrived(jnp.int32(PAIR))
+            carry[...] = carry[...] * decay_block * decay_block + got[PAIR].astype(F32)
+
+        @pl.loop(jnp.where(z > PAIR, PAIR + 1, pick(HEAD, z) + 1), z)
         def _(source):
-            remote(
-                own_msg, got.at[source], e_send.at[0], c_recv.at[source], {"ctx": z}
-            ).wait_recv()
+            @pl.when(source != PAIR - 1)
+            def _():
+                arrived(source)
+
             carry[...] = carry[...] * decay_block + got[source].astype(F32)
 
-    @pl.when(sends_prefix)
+    def send_whole(k, targets):
+        for j in reversed(targets):
+            message(pre_msg, p_send, j).start()
+
+    @pl.when(z == PAIR)
+    def _():
+        arrived(jnp.int32(PAIR - 1))
+        pre_msg[...] = (
+            state[...] + decay_block * got[PAIR - 1].astype(F32)
+        ).astype(BF16)
+        send_whole(PAIR, [j for j in range(blocks) if PAIR in whole[j]])
+
+    @pl.when(heads)
     def _():
         receive_carry()
         pre_msg[...] = (state[...] + decay_block * carry[...]).astype(BF16)
-        for j in range(1, blocks):
-
-            @pl.when(z == FIRST[j])
+        for k in sorted({k for j in whole for k in whole[j]} - {PAIR}):
+
+            @pl.when(z == k)
             def _():
-                remote(
-                    pre_msg,
-                    got.at[z],
-                    p_send.at[j],
-                    c_recv.at[z],
-                    {"ctx": jnp.int32(j)},
-                ).start()
+                targets = [j for j in range(blocks) if k in whole[j]]
+                send_whole(k, [j for j in targets if late.get(j) != k])
+                if k in LATE and k != HUB:
+                    pl.semaphore_wait(ready, len(LATE[k]))
+                    send_whole(k, [j for j in targets if late.get(j) == k])
+
+    def hub_step():
+        @pl.when(z == HUB)
+        def _():
+            total = None
+            for source in range(HUB_HEAD, HUB_LAST + 1):
+                arrived(jnp.int32(source))
+                block = got[source].astype(F32)
+                total = block if total is None else total * decay_block + block
+            hub_msg[...] = total.astype(BF16)
+            pl.semaphore_wait(ready, len(HUB_TO))
+            for j in reversed(HUB_TO):
+                message(hub_msg, p_send, j).start()
 
     for half in range(2):
         lanes = pl.ds(half * (channels // 2), channels // 2)
@@ -203,7 +305,7 @@
         )
     loads[4].wait()
 
-    @pl.when(jnp.logical_not(sends_prefix))
+    @pl.when(jnp.logical_not(heads))
     def _():
         receive_carry()
 
@@ -235,16 +337,55 @@
     loads[6].wait()
     place = (x, y)
     band = SIDE * SUB
+    cut = band // 2
     order = (2, 1, 3)
+    pieces = [(c, h) for c in range(CHUNKS) for h in range(2)]
+
+    def rows_of(c, h, shift, low=0, count=band):
+        target = (place[h] + shift) % SIDE
+        return part.at[c, h, pl.ds(pl.multiple_of(target * band + low, cut), count)]
+
+    def project(c, h):
+        columns = pl.ds((h * CHUNKS + c) * width, width)
+        part[c, h] = jnp.dot(
+            gated[h], weight[:, columns], preferred_element_type=F32
+        ).astype(BF16)
 
     def first_copy(c, h, shift):
-        target = (place[h] + shift) % SIDE
         return remote(
-            part.at[c, h, pl.ds(pl.multiple_of(target * band, band), band)],
+            rows_of(c, h, shift),
             part_in.at[c, h, shift - 1],
             r1_send.at[c, h, shift - 1],
             r1_recv.at[c, h, shift - 1],
             line(h, shift),
+        )
+
+    def opposite_copy(c, h, side):
+        return remote(
+            rows_of(c, h, 2, side * cut, cut),
+            relay_in.at[c, h, side],
+            a_send.at[c, h, side],
+            a_recv.at[c, h, side],
+            line(h, (1, SIDE - 1)[side]),
+        )
+
+    def direct_copy(c, h, side):
+        low = (1 - side) * cut
+        return remote(
+            rows_of(c, h, (1, SIDE - 1)[side], low, cut),
+            part_in.at[c, h, side, pl.ds(low, cut)],
+            r1_send.at[c, h, side],
+            r1_recv.at[c, h, side],
+            line(h, (1, SIDE - 1)[side]),
+        )
+
+    def relay_copy(c, h, side):
+        return remote(
+            relay_out.at[c, h, side],
+            part_in.at[c, h, side, pl.ds(side * cut, cut)],
+            r1_send.at[c, h, 2 + side],
+            r1_recv.at[c, h, 2 + side],
+            line(h, (1, SIDE - 1)[side]),
         )
 
     def second_copy(c, h, shift):
@@ -257,65 +398,108 @@
             line(1 - h, shift),
         )
 
-    for c in range(CHUNKS):
-        for h in range(2):
-            columns = pl.ds((h * CHUNKS + c) * width, width)
-            part[c, h] = jnp.dot(
-                gated[h], weight[:, columns], preferred_element_type=F32
+    def second_phase(c, h, total):
+        for i in range(SIDE):
+            rows = total[SUB * i : SUB * (i + 1)]
+            half_sum[c, h, i] = jnp.concatenate(
+                [rows[:, : width // 2], rows[:, width // 2 :]], axis=0
             ).astype(BF16)
-            for shift in order:
-                first_copy(c, h, shift).start()
-
-    for c in range(CHUNKS):
-        for h in range(2):
-            mine = pl.ds(pl.multiple_of(place[h] * band, band), band)
-            total = part[c, h, mine].astype(F32)
+        for shift in order:
+            second_copy(c, h, shift).start()
+
+    @pl.when(core == 0)
+    def _():
+        for c in range(CHUNKS):
+            for h in range(2):
+                project(c, h)
+                first_copy(c, h, 2).start()
+            for h in range(2):
+                for shift in (1, 3):
+                    first_copy(c, h, shift).start()
+        hub_step()
+        for c, h in pieces:
+            total = rows_of(c, h, 0)[...].astype(F32)
             for shift in order:
                 first_copy(c, h, shift).wait_recv()
                 total = total + part_in[c, h, shift - 1].astype(F32)
-            for i in range(SIDE):
-                rows = total[SUB * i : SUB * (i + 1)]
-                half_sum[c, h, i] = jnp.concatenate(
-                    [rows[:, : width // 2], rows[:, width // 2 :]], axis=0
+            second_phase(c, h, total)
+
+    @pl.when(core == 1)
+    def _():
+        for c, h in pieces:
+            project(c, h)
+            for side in range(2):
+                opposite_copy(c, h, side).start()
+        for c, h in pieces:
+            for side in range(2):
+                direct_copy(c, h, side).start()
+        hub_step()
+        for c, h in pieces:
+            for side in range(2):
+                opposite_copy(c, h, side).wait_recv()
+                mine = rows_of(c, h, (1, SIDE - 1)[side], side * cut, cut)
+                relay_out[c, h, side] = (
+                    mine[...].astype(F32) + relay_in[c, h, side].astype(F32)
                 ).astype(BF16)
-            for shift in order:
-                second_copy(c, h, shift).start()
-
-    for c in range(CHUNKS):
-        for h in range(2):
-            total = half_sum[c, h, place[1 - h]].astype(F32)
-            for shift in order:
-                second_copy(c, h, shift).wait_recv()
-                total = total + half_in[c, h, shift - 1].astype(F32)
-            start = (h * CHUNKS + c) * width
-            out_ref[:, pl.ds(start, width // 2)] = total[:SUB].astype(BF16)
-            out_ref[:, pl.ds(start + width // 2, width // 2)] = total[SUB:].astype(BF16)
-
-    for c in range(CHUNKS):
-        for h in range(2):
+                relay_copy(c, h, side).start()
+        for c, h in pieces:
+            for side in range(2):
+                direct_copy(c, h, side).wait_recv()
+                relay_copy(c, h, side).wait_recv()
+            second_phase(
+                c,
+                h,
+                rows_of(c, h, 0)[...].astype(F32)
+                + part_in[c, h, 0].astype(F32)
+                + part_in[c, h, 1].astype(F32),
+            )
+
+    for c, h in pieces:
+        total = half_sum[c, h, place[1 - h]].astype(F32)
+        for shift in order:
+            second_copy(c, h, shift).wait_recv()
+            total = total + half_in[c, h, shift - 1].astype(F32)
+        start = (h * CHUNKS + c) * width
+        out_ref[:, pl.ds(start, width // 2)] = total[:SUB].astype(BF16)
+        out_ref[:, pl.ds(start + width // 2, width // 2)] = total[SUB:].astype(BF16)
+
+    @pl.when(core == 0)
+    def _():
+        for c, h in pieces:
             for shift in order:
                 first_copy(c, h, shift).wait_send()
-                second_copy(c, h, shift).wait_send()
+
+    @pl.when(core == 1)
+    def _():
+        for c, h in pieces:
+            for side in range(2):
+                opposite_copy(c, h, side).wait_send()
+                direct_copy(c, h, side).wait_send()
+                relay_copy(c, h, side).wait_send()
+
+    for c, h in pieces:
+        for shift in order:
+            second_copy(c, h, shift).wait_send()
     for j in range(1, blocks):
-
-        @pl.when(jnp.logical_and(z > FIRST[j], z < j))
-        def _():
-            remote(
-                own_msg, got.at[z], e_send.at[j], c_recv.at[z], {"ctx": jnp.int32(j)}
-            ).wait_send()
-
-        @pl.when(z == FIRST[j])
-        def _():
-            remote(
-                pre_msg, got.at[z], p_send.at[j], c_recv.at[z], {"ctx": jnp.int32(j)}
-            ).wait_send()
+        if plain[j]:
+
+            @pl.when(among(plain[j]))
+            def _():
+                message(own_msg, e_send, j).wait_send()
+
+        senders = whole[j] + ([HUB] if j in HUB_TO else [])
+        if senders:
+
+            @pl.when(among(senders))
+            def _():
+                message(pre_msg, p_send, j).wait_send()
 
 
 def on_device(queries, keys, values, residues, decays, skip, out_weight):
     tokens, channels = keys.shape
     modes = residues.shape[1]
     features = out_weight.shape[1]
-    blocks = len(FIRST)
+    blocks = len(HEAD)
     width = features // (2 * CHUNKS)
     band = SIDE * SUB
     hbm = pl.BlockSpec(memory_space=pltpu.HBM)
@@ -342,20 +526,26 @@
             pltpu.VMEM((modes, channels), F32),
             pltpu.VMEM((modes, channels), BF16),
             pltpu.VMEM((modes, channels), BF16),
+            pltpu.VMEM((modes, channels), BF16),
             pltpu.VMEM((blocks, modes, channels), BF16),
             pltpu.VMEM((2, tokens, channels), BF16),
             pltpu.VMEM((CHUNKS, 2, tokens, width), BF16),
             pltpu.VMEM((CHUNKS, 2, SIDE - 1, band, width), BF16),
+            pltpu.VMEM((CHUNKS, 2, 2, band // 2, width), BF16),
+            pltpu.VMEM((CHUNKS, 2, 2, band // 2, width), BF16),
             pltpu.VMEM((CHUNKS, 2, SIDE, 2 * SUB, width // 2), BF16),
             pltpu.VMEM((CHUNKS, 2, SIDE - 1, 2 * SUB, width // 2), BF16),
             dma((7,)),
             dma((blocks,)),
             dma((blocks,)),
             dma((blocks,)),
+            dma((CHUNKS, 2, 2)),
+            dma((CHUNKS, 2, 2)),
+            dma((CHUNKS, 2, 4)),
+            dma((CHUNKS, 2, 4)),
             dma((CHUNKS, 2, SIDE - 1)),
             dma((CHUNKS, 2, SIDE - 1)),
-            dma((CHUNKS, 2, SIDE - 1)),
-            dma((CHUNKS, 2, SIDE - 1)),
+            pltpu.SemaphoreType.REGULAR,
         ],
         compiler_params=pltpu.CompilerParams(
             collective_id=0, has_side_effects=True, vmem_limit_bytes=60 << 20

time: 30 us -> 27.5 us (0.917)
  the two profiles are of different devices: /device:TPU:448 before, /device:TPU:480 now
where the time goes in v3:
time: 27.5 us; the launch traced here: 27.4 us
  Pallas kernels  26.8 us (97%)
  local copies, waits for them, and re-layouts  0.63 us (2%)
    pallas_call x1, Pallas kernels, on_device(): pl.pallas_call(operator_kernel, out_shape=pltpu.VMEM((SUB, features), BF1...  26.8 us
    unnamed x1, local copies, waits for them, and re-layouts  0.63 us

profile of v3, /device:TPU:480, one launch (start us, length us, event | category | flops | bytes accessed | tf_op | source)
XLA Modules:
  0.0 27.4 jit_solution(4856477049996794091)
XLA Ops:
  0.0 26.8 %shard_map.73 = bf16[8,4096]{1,0:T(8,128)(2,1)S(1)} custom-call(bf16[128,256]{1,0:T(8,128)(2,1)} %q_hbm.1, bf16[128,256]{1,0:T(8,128)(2,1)} %k_hbm.1, bf16[128,256]{1,0:T(8,128)(2,1)} %v_hbm.1, f32[16,256]{1,0:T(8,128)} %bitcast.3, f32[16,256]{1,0:T(8,128)} %bitcast.4, f32[1,256]{1,0:T(1,128)} %bitcast.5, bf16[256,4096]{1,0:T(8,128)(2,1)} %w_hbm.1), custom_call_target="tpu_custom_call" | custom-call | tf_op jit(solution)/shard_map/pallas_call | solution.py:507
  26.8 0.6 %copy.9 = bf16[8,4096]{1,0:T(8,128)(2,1)} copy(bf16[8,4096]{1,0:T(8,128)(2,1)S(1)} %shard_map.73) | data formatting | bytes 131072

commit v4 on v3

--- a/solution.py
+++ b/solution.py
@@ -13,11 +13,11 @@
 
 SIDE = 4
 SUB = 8
-HEAD = (0, 0, 1, 0, 3, 3, 3, 6, 6, 6, 6, 6, 1, 1, 1, 1)
-HUB, HUB_HEAD, HUB_LAST, HUB_TO = 1, 3, 6, (12, 13, 14, 15)
+HEAD = (0, 0, 1, 0, 3, 3, 3, 6, 6, 6, 6, 6, 0, 0, 0, 0)
+HUB, HUB_HEAD, HUB_LAST, HUB_TO = 0, 3, 6, (12, 13, 14, 15)
 PAIR = 8
 LATE = {HUB: HUB_TO, 6: (8, 9, 10, 11)}
-CHUNKS = 2
+LEVELS = 2
 
 
 def pick(table, index):
@@ -58,6 +58,7 @@
     kern,
     conv,
     gain,
+    lead,
     step8,
     state,
     carry,
@@ -88,7 +89,8 @@
     tokens, channels = k_in.shape
     groups = tokens // SUB
     modes = res.shape[0]
-    width = part.shape[3]
+    width = part.shape[4]
+    split = width // 2
     z = lax.axis_index("ctx")
     tp = lax.axis_index("tp")
     core = lax.axis_index("dp")
@@ -125,7 +127,7 @@
     def among(members):
         return functools.reduce(jnp.logical_or, [z == i for i in sorted(members)])
 
-    heads = among({k for j in range(1, blocks) for k in whole[j]} - {PAIR})
+    heads = among({k for j in range(blocks) for k in whole[j]} - {PAIR})
     barrier = pltpu.get_barrier_semaphore()
 
     for source in range(blocks):
@@ -189,6 +191,7 @@
         a8 = jnp.exp(-float(SUB) * rate)
         step8[s] = a8
         gain[s] = amp * jnp.exp(-rate * row)
+        lead[s] = amp * jnp.exp(-rate * (row + 1.0))
         total = xpad[pl.ds(SUB, SUB), :]
         for m in range(1, groups):
             total = total * a8 + xpad[pl.ds(SUB * (m + 1), SUB), :]
@@ -219,34 +222,42 @@
             own_msg, got.at[source], e_send.at[0], c_recv.at[source], {"ctx": z}
         ).wait_recv()
 
-    for j in reversed(range(1, blocks)):
+    for j in reversed(range(blocks)):
         if plain[j]:
 
             @pl.when(among(plain[j]))
             def _():
                 message(own_msg, e_send, j).start()
 
+    head = pick(HEAD, z)
+    behind = jnp.where(z > PAIR, z - 1 - HUB_LAST, z - 1 - head)
+    head_decay = jnp.exp(
+        -float(tokens) * jnp.maximum(behind, 0).astype(F32) * dec[...]
+    )
+    pair_decay = jnp.exp(
+        -float(tokens) * jnp.maximum(z - 1 - PAIR, 0).astype(F32) * dec[...]
+    )
+
     def receive_carry():
         carry[...] = jnp.zeros_like(carry)
 
-        @pl.when(z > 0)
-        def _():
-            head = pick(HEAD, z)
-            arrived(head)
-            carry[...] = got[head].astype(F32)
-
-        @pl.when(z > PAIR)
-        def _():
-            arrived(jnp.int32(PAIR))
-            carry[...] = carry[...] * decay_block * decay_block + got[PAIR].astype(F32)
-
-        @pl.loop(jnp.where(z > PAIR, PAIR + 1, pick(HEAD, z) + 1), z)
+        @pl.loop(jnp.where(z > PAIR, PAIR, head) + 1, z)
         def _(source):
             @pl.when(source != PAIR - 1)
             def _():
                 arrived(source)
 
             carry[...] = carry[...] * decay_block + got[source].astype(F32)
+
+        @pl.when(z > PAIR)
+        def _():
+            arrived(jnp.int32(PAIR))
+            carry[...] += pair_decay * got[PAIR].astype(F32)
+
+        @pl.when(z > 0)
+        def _():
+            arrived(head)
+            carry[...] += head_decay * got[head].astype(F32)
 
     def send_whole(k, targets):
         for j in reversed(targets):
@@ -311,13 +322,11 @@
 
     for half in range(2):
         lanes = pl.ds(half * (channels // 2), channels // 2)
-        base = []
-        for s in range(modes):
-            a1 = jnp.exp(-dec[pl.ds(s, 1), lanes])
-            base.append(
-                gain[s, :, lanes]
-                * jnp.broadcast_to(a1 * carry[pl.ds(s, 1), lanes], (SUB, channels // 2))
-            )
+        base = [
+            lead[s, :, lanes]
+            * jnp.broadcast_to(carry[pl.ds(s, 1), lanes], (SUB, channels // 2))
+            for s in range(modes)
+        ]
         for m in range(groups):
             here = pl.ds(SUB * m, SUB)
             conv[here, lanes] += sum(base[1:], base[0])
@@ -337,150 +346,152 @@
     loads[6].wait()
     place = (x, y)
     band = SIDE * SUB
-    cut = band // 2
+    cut = band // LEVELS
     order = (2, 1, 3)
-    pieces = [(c, h) for c in range(CHUNKS) for h in range(2)]
-
-    def rows_of(c, h, shift, low=0, count=band):
-        target = (place[h] + shift) % SIDE
-        return part.at[c, h, pl.ds(pl.multiple_of(target * band + low, cut), count)]
-
-    def project(c, h):
-        columns = pl.ds((h * CHUNKS + c) * width, width)
-        part[c, h] = jnp.dot(
-            gated[h], weight[:, columns], preferred_element_type=F32
-        ).astype(BF16)
-
-    def first_copy(c, h, shift):
+    steps = (1, SIDE - 1)
+    pieces = [(r, h) for r in range(LEVELS) for h in range(2)]
+
+    def at(h, shift):
+        return (place[h] + shift) % SIDE
+
+    def project(h):
+        for side in range(2):
+            value = jnp.dot(
+                gated[h],
+                weight[:, pl.ds(h * width + side * split, split)],
+                preferred_element_type=F32,
+            ).astype(BF16)
+            for r in range(LEVELS):
+                for i in range(SIDE):
+                    start = i * band + r * cut
+                    part[r, h, i, :, pl.ds(side * split, split)] = value[
+                        start : start + cut
+                    ]
+
+    def first_copy(r, h, shift):
         return remote(
-            rows_of(c, h, shift),
-            part_in.at[c, h, shift - 1],
-            r1_send.at[c, h, shift - 1],
-            r1_recv.at[c, h, shift - 1],
+            part.at[r, h, at(h, shift)],
+            part_in.at[r, h, shift - 1],
+            r1_send.at[r, h, shift - 1],
+            r1_recv.at[r, h, shift - 1],
             line(h, shift),
         )
 
-    def opposite_copy(c, h, side):
+    def opposite_copy(r, h, side):
         return remote(
-            rows_of(c, h, 2, side * cut, cut),
-            relay_in.at[c, h, side],
-            a_send.at[c, h, side],
-            a_recv.at[c, h, side],
-            line(h, (1, SIDE - 1)[side]),
-        )
-
-    def direct_copy(c, h, side):
-        low = (1 - side) * cut
+            part.at[r, h, at(h, 2), :, pl.ds(side * split, split)],
+            relay_in.at[r, h, side],
+            a_send.at[r, h, side],
+            a_recv.at[r, h, side],
+            line(h, steps[side]),
+        )
+
+    def direct_copy(r, h, side):
+        columns = pl.ds((1 - side) * split, split)
         return remote(
-            rows_of(c, h, (1, SIDE - 1)[side], low, cut),
-            part_in.at[c, h, side, pl.ds(low, cut)],
-            r1_send.at[c, h, side],
-            r1_recv.at[c, h, side],
-            line(h, (1, SIDE - 1)[side]),
-        )
-
-    def relay_copy(c, h, side):
+            part.at[r, h, at(h, steps[side]), :, columns],
+            part_in.at[r, h, side, :, columns],
+            r1_send.at[r, h, side],
+            r1_recv.at[r, h, side],
+            line(h, steps[side]),
+        )
+
+    def relay_copy(r, h, side):
         return remote(
-            relay_out.at[c, h, side],
-            part_in.at[c, h, side, pl.ds(side * cut, cut)],
-            r1_send.at[c, h, 2 + side],
-            r1_recv.at[c, h, 2 + side],
-            line(h, (1, SIDE - 1)[side]),
-        )
-
-    def second_copy(c, h, shift):
-        target = (place[1 - h] + shift) % SIDE
+            relay_out.at[r, h, side],
+            part_in.at[r, h, side, :, pl.ds(side * split, split)],
+            r1_send.at[r, h, 2 + side],
+            r1_recv.at[r, h, 2 + side],
+            line(h, steps[side]),
+        )
+
+    def second_copy(h, target, shift):
         return remote(
-            half_sum.at[c, h, target],
-            half_in.at[c, h, shift - 1],
-            r2_send.at[c, h, shift - 1],
-            r2_recv.at[c, h, shift - 1],
+            half_sum.at[h, target],
+            half_in.at[h, shift - 1],
+            r2_send.at[h, shift - 1],
+            r2_recv.at[h, shift - 1],
             line(1 - h, shift),
         )
 
-    def second_phase(c, h, total):
-        for i in range(SIDE):
+    def second_phase(r, h, total):
+        for i in range(LEVELS):
             rows = total[SUB * i : SUB * (i + 1)]
-            half_sum[c, h, i] = jnp.concatenate(
-                [rows[:, : width // 2], rows[:, width // 2 :]], axis=0
+            target = LEVELS * r + i
+            half_sum[h, target] = jnp.concatenate(
+                [rows[:, :split], rows[:, split:]], axis=0
             ).astype(BF16)
-        for shift in order:
-            second_copy(c, h, shift).start()
+
+            @pl.when(place[1 - h] != target)
+            def _():
+                second_copy(h, target, (target - place[1 - h] + SIDE) % SIDE).start()
 
     @pl.when(core == 0)
     def _():
-        for c in range(CHUNKS):
+        for h in range(2):
+            project(h)
+            first_copy(0, h, 2).start()
+        for r in range(LEVELS):
             for h in range(2):
-                project(c, h)
-                first_copy(c, h, 2).start()
+                if r > 0:
+                    first_copy(r, h, 2).start()
             for h in range(2):
                 for shift in (1, 3):
-                    first_copy(c, h, shift).start()
+                    first_copy(r, h, shift).start()
         hub_step()
-        for c, h in pieces:
-            total = rows_of(c, h, 0)[...].astype(F32)
+        for r, h in pieces:
+            total = part[r, h, place[h]].astype(F32)
             for shift in order:
-                first_copy(c, h, shift).wait_recv()
-                total = total + part_in[c, h, shift - 1].astype(F32)
-            second_phase(c, h, total)
+                first_copy(r, h, shift).wait_recv()
+                total = total + part_in[r, h, shift - 1].astype(F32)
+            second_phase(r, h, total)
 
     @pl.when(core == 1)
     def _():
-        for c, h in pieces:
-            project(c, h)
+        for h in range(2):
+            project(h)
+            for r in range(LEVELS):
+                for side in range(2):
+                    opposite_copy(r, h, side).start()
+        for r, h in pieces:
             for side in range(2):
-                opposite_copy(c, h, side).start()
-        for c, h in pieces:
+                direct_copy(r, h, side).start()
+        hub_step()
+        for r, h in pieces:
             for side in range(2):
-                direct_copy(c, h, side).start()
-        hub_step()
-        for c, h in pieces:
+                opposite_copy(r, h, side).wait_recv()
+                mine = part[r, h, at(h, steps[side]), :, pl.ds(side * split, split)]
+                relay_out[r, h, side] = (
+                    mine.astype(F32) + relay_in[r, h, side].astype(F32)
+                ).astype(BF16)
+                relay_copy(r, h, side).start()
+        for r, h in pieces:
             for side in range(2):
-                opposite_copy(c, h, side).wait_recv()
-                mine = rows_of(c, h, (1, SIDE - 1)[side], side * cut, cut)
-                relay_out[c, h, side] = (
-                    mine[...].astype(F32) + relay_in[c, h, side].astype(F32)
-                ).astype(BF16)
-                relay_copy(c, h, side).start()
-        for c, h in pieces:
-            for side in range(2):
-                direct_copy(c, h, side).wait_recv()
-                relay_copy(c, h, side).wait_recv()
+                direct_copy(r, h, side).wait_recv()
+                relay_copy(r, h, side).wait_recv()
             second_phase(
-                c,
+                r,
                 h,
-                rows_of(c, h, 0)[...].astype(F32)
-                + part_in[c, h, 0].astype(F32)
-                + part_in[c, h, 1].astype(F32),
+                part[r, h, place[h]].astype(F32)
+                + part_in[r, h, 0].astype(F32)
+                + part_in[r, h, 1].astype(F32),
             )
-
-    for c, h in pieces:
-        total = half_sum[c, h, place[1 - h]].astype(F32)
-        for shift in order:
-            second_copy(c, h, shift).wait_recv()
-            total = total + half_in[c, h, shift - 1].astype(F32)
-        start = (h * CHUNKS + c) * width
-        out_ref[:, pl.ds(start, width // 2)] = total[:SUB].astype(BF16)
-        out_ref[:, pl.ds(start + width // 2, width // 2)] = total[SUB:].astype(BF16)
 
     @pl.when(core == 0)
     def _():
-        for c, h in pieces:
+        for r, h in pieces:
             for shift in order:
-                first_copy(c, h, shift).wait_send()
+                first_copy(r, h, shift).wait_send()
 
     @pl.when(core == 1)
     def _():
-        for c, h in pieces:
+        for r, h in pieces:
             for side in range(2):
-                opposite_copy(c, h, side).wait_send()
-                direct_copy(c, h, side).wait_send()
-                relay_copy(c, h, side).wait_send()
-
-    for c, h in pieces:
-        for shift in order:
-            second_copy(c, h, shift).wait_send()
-    for j in range(1, blocks):
+                opposite_copy(r, h, side).wait_send()
+                direct_copy(r, h, side).wait_send()
+                relay_copy(r, h, side).wait_send()
+
+    for j in range(blocks):
         if plain[j]:
 
             @pl.when(among(plain[j]))
@@ -493,6 +504,20 @@
             @pl.when(among(senders))
             def _():
                 message(pre_msg, p_send, j).wait_send()
+
+    for h in range(2):
+        for shift in order:
+            second_copy(h, at(1 - h, shift), shift).wait_send()
+
+    for h in range(2):
+        total = half_sum[h, place[1 - h]].astype(F32)
+        for shift in order:
+            second_copy(h, place[1 - h], shift).wait_recv()
+            total = total + half_in[h, shift - 1].astype(F32)
+        for side in range(2):
+            out_ref[:, pl.ds(h * width + side * split, split)] = total[
+                SUB * side : SUB * (side + 1)
+            ].astype(BF16)
 
 
 def on_device(queries, keys, values, residues, decays, skip, out_weight):
@@ -500,7 +525,7 @@
     modes = residues.shape[1]
     features = out_weight.shape[1]
     blocks = len(HEAD)
-    width = features // (2 * CHUNKS)
+    width = features // 2
     band = SIDE * SUB
     hbm = pl.BlockSpec(memory_space=pltpu.HBM)
     dma = pltpu.SemaphoreType.DMA
@@ -522,6 +547,7 @@
             pltpu.VMEM((tokens, channels), F32),
             pltpu.VMEM((modes, SUB, channels), F32),
             pltpu.VMEM((modes, SUB, channels), F32),
+            pltpu.VMEM((modes, SUB, channels), F32),
             pltpu.VMEM((modes, channels), F32),
             pltpu.VMEM((modes, channels), F32),
             pltpu.VMEM((modes, channels), BF16),
@@ -529,22 +555,22 @@
             pltpu.VMEM((modes, channels), BF16),
             pltpu.VMEM((blocks, modes, channels), BF16),
             pltpu.VMEM((2, tokens, channels), BF16),
-            pltpu.VMEM((CHUNKS, 2, tokens, width), BF16),
-            pltpu.VMEM((CHUNKS, 2, SIDE - 1, band, width), BF16),
-            pltpu.VMEM((CHUNKS, 2, 2, band // 2, width), BF16),
-            pltpu.VMEM((CHUNKS, 2, 2, band // 2, width), BF16),
-            pltpu.VMEM((CHUNKS, 2, SIDE, 2 * SUB, width // 2), BF16),
-            pltpu.VMEM((CHUNKS, 2, SIDE - 1, 2 * SUB, width // 2), BF16),
+            pltpu.VMEM((LEVELS, 2, SIDE, band // LEVELS, width), BF16),
+            pltpu.VMEM((LEVELS, 2, SIDE - 1, band // LEVELS, width), BF16),
+            pltpu.VMEM((LEVELS, 2, 2, band // LEVELS, width // 2), BF16),
+            pltpu.VMEM((LEVELS, 2, 2, band // LEVELS, width // 2), BF16),
+            pltpu.VMEM((2, SIDE, 2 * SUB, width // 2), BF16),
+            pltpu.VMEM((2, SIDE - 1, 2 * SUB, width // 2), BF16),
             dma((7,)),
             dma((blocks,)),
             dma((blocks,)),
             dma((blocks,)),
-            dma((CHUNKS, 2, 2)),
-            dma((CHUNKS, 2, 2)),
-            dma((CHUNKS, 2, 4)),
-            dma((CHUNKS, 2, 4)),
-            dma((CHUNKS, 2, SIDE - 1)),
-            dma((CHUNKS, 2, SIDE - 1)),
+            dma((LEVELS, 2, 2)),
+            dma((LEVELS, 2, 2)),
+            dma((LEVELS, 2, 4)),
+            dma((LEVELS, 2, 4)),
+            dma((2, SIDE - 1)),
+            dma((2, SIDE - 1)),
             pltpu.SemaphoreType.REGULAR,
         ],
         compiler_params=pltpu.CompilerParams(

time: 27.5 us -> 26.1 us (0.949)
  Pallas kernels: 26.8 us -> 25.3 us
    pallas_call x1, Pallas kernels: 26.8 us -> 25.3 us  [on_device(): pl.pallas_call(operator_kernel, out_shape=pltpu.VMEM((SUB, features), BF1...]
where the time goes in v4:
time: 26.1 us; the launch traced here: 25.9 us
  Pallas kernels  25.3 us (97%)
  local copies, waits for them, and re-layouts  0.63 us (2%)
    pallas_call x1, Pallas kernels, on_device(): pl.pallas_call(operator_kernel, out_shape=pltpu.VMEM((SUB, features), BF1...  25.3 us
    unnamed x1, local copies, waits for them, and re-layouts  0.63 us

profile of v4, /device:TPU:480, one launch (start us, length us, event | category | flops | bytes accessed | tf_op | source)
XLA Modules:
  0.0 25.9 jit_solution(16423044766957668685)
XLA Ops:
  0.0 25.3 %shard_map.73 = bf16[8,4096]{1,0:T(8,128)(2,1)S(1)} custom-call(bf16[128,256]{1,0:T(8,128)(2,1)} %q_hbm.1, bf16[128,256]{1,0:T(8,128)(2,1)} %k_hbm.1, bf16[128,256]{1,0:T(8,128)(2,1)} %v_hbm.1, f32[16,256]{1,0:T(8,128)} %bitcast.3, f32[16,256]{1,0:T(8,128)} %bitcast.4, f32[1,256]{1,0:T(1,128)} %bitcast.5, bf16[256,4096]{1,0:T(8,128)(2,1)} %w_hbm.1), custom_call_target="tpu_custom_call" | custom-call | tf_op jit(solution)/shard_map/pallas_call | solution.py:532
  25.3 0.6 %copy.9 = bf16[8,4096]{1,0:T(8,128)(2,1)} copy(bf16[8,4096]{1,0:T(8,128)(2,1)S(1)} %shard_map.73) | data formatting | bytes 131072

commit v5 on v4

--- a/solution.py
+++ b/solution.py
@@ -84,6 +84,7 @@
     r2_send,
     r2_recv,
     ready,
+    turn,
 ):
     blocks = len(HEAD)
     tokens, channels = k_in.shape
@@ -125,12 +126,25 @@
     )
 
     def among(members):
-        return functools.reduce(jnp.logical_or, [z == i for i in sorted(members)])
+        members = sorted(members)
+        spans = []
+        for i in members:
+            if spans and spans[-1][1] == i - 1:
+                spans[-1][1] = i
+            else:
+                spans.append([i, i])
+        return functools.reduce(
+            jnp.logical_or,
+            [
+                z == low if low == high else jnp.logical_and(z >= low, z <= high)
+                for low, high in spans
+            ],
+        )
 
     heads = among({k for j in range(blocks) for k in whole[j]} - {PAIR})
     barrier = pltpu.get_barrier_semaphore()
 
-    for source in range(blocks):
+    for source in (*range(PAIR, blocks), *range(PAIR)):
         if any(source in greeted[j] for j in range(blocks)):
 
             @pl.when(among([j for j in range(blocks) if source in greeted[j]]))
@@ -159,6 +173,12 @@
             pl.semaphore_signal(
                 barrier, inc=1, device_id=line(axis, shift), device_id_type=MESH
             )
+
+    @pl.when(core == 1)
+    def _():
+        pl.semaphore_signal(
+            barrier, inc=1, device_id={"dp": jnp.int32(0)}, device_id_type=MESH
+        )
 
     loads = [
         pltpu.make_async_copy(src, dst, in_sem.at[i])
@@ -200,7 +220,7 @@
     own_msg[...] = state[...].astype(BF16)
     decay_block = jnp.exp(-float(tokens) * dec[...])
 
-    pl.semaphore_wait(barrier, 2 * (SIDE - 1) + expected)
+    pl.semaphore_wait(barrier, 2 * (SIDE - 1) + expected + 1 - core)
     for source, group in LATE.items():
 
         @pl.when(among(group))
@@ -222,6 +242,18 @@
             own_msg, got.at[source], e_send.at[0], c_recv.at[source], {"ctx": z}
         ).wait_recv()
 
+    def send_whole(k, targets):
+        for j in reversed(targets):
+            message(pre_msg, p_send, j).start()
+
+    @pl.when(z == PAIR)
+    def _():
+        arrived(jnp.int32(PAIR - 1))
+        pre_msg[...] = (
+            state[...] + decay_block * got[PAIR - 1].astype(F32)
+        ).astype(BF16)
+        send_whole(PAIR, [j for j in range(blocks) if PAIR in whole[j]])
+
     for j in reversed(range(blocks)):
         if plain[j]:
 
@@ -258,18 +290,6 @@
         def _():
             arrived(head)
             carry[...] += head_decay * got[head].astype(F32)
-
-    def send_whole(k, targets):
-        for j in reversed(targets):
-            message(pre_msg, p_send, j).start()
-
-    @pl.when(z == PAIR)
-    def _():
-        arrived(jnp.int32(PAIR - 1))
-        pre_msg[...] = (
-            state[...] + decay_block * got[PAIR - 1].astype(F32)
-        ).astype(BF16)
-        send_whole(PAIR, [j for j in range(blocks) if PAIR in whole[j]])
 
     @pl.when(heads)
     def _():
@@ -327,21 +347,21 @@
             * jnp.broadcast_to(carry[pl.ds(s, 1), lanes], (SUB, channels // 2))
             for s in range(modes)
         ]
+        rows = []
         for m in range(groups):
             here = pl.ds(SUB * m, SUB)
-            conv[here, lanes] += sum(base[1:], base[0])
+            rows.append(
+                q_in[here, lanes].astype(F32)
+                * (conv[here, lanes] + sum(base[1:], base[0]))
+            )
             if m + 1 < groups:
                 base = [b * step8[s, :, lanes] for s, b in enumerate(base)]
-    product = q_in[...].astype(F32) * conv[...]
-    gated[0] = product.astype(BF16)
-    gated[1] = jnp.concatenate(
-        [
-            product[SUB * (SIDE * i + j) : SUB * (SIDE * i + j + 1)]
-            for j in range(SIDE)
-            for i in range(SIDE)
-        ],
-        axis=0,
-    ).astype(BF16)
+        turned = [rows[SIDE * i + j] for j in range(SIDE) for i in range(SIDE)]
+        for h, ordered in enumerate((rows, turned)):
+            for m in range(0, groups, 2):
+                gated[h, pl.ds(SUB * m, 2 * SUB), lanes] = jnp.concatenate(
+                    ordered[m : m + 2], axis=0
+                ).astype(BF16)
 
     loads[6].wait()
     place = (x, y)
@@ -439,6 +459,12 @@
                 for shift in (1, 3):
                     first_copy(r, h, shift).start()
         hub_step()
+        for r, h in pieces:
+            for shift in order:
+                first_copy(r, h, shift).wait_send()
+        pl.semaphore_signal(
+            turn, inc=1, device_id={"dp": jnp.int32(1)}, device_id_type=MESH
+        )
         for r, h in pieces:
             total = part[r, h, place[h]].astype(F32)
             for shift in order:
@@ -465,6 +491,7 @@
                     mine.astype(F32) + relay_in[r, h, side].astype(F32)
                 ).astype(BF16)
                 relay_copy(r, h, side).start()
+        pl.semaphore_wait(turn, 1)
         for r, h in pieces:
             for side in range(2):
                 direct_copy(r, h, side).wait_recv()
@@ -476,12 +503,6 @@
                 + part_in[r, h, 0].astype(F32)
                 + part_in[r, h, 1].astype(F32),
             )
-
-    @pl.when(core == 0)
-    def _():
-        for r, h in pieces:
-            for shift in order:
-                first_copy(r, h, shift).wait_send()
 
     @pl.when(core == 1)
     def _():
@@ -572,6 +593,7 @@
             dma((2, SIDE - 1)),
             dma((2, SIDE - 1)),
             pltpu.SemaphoreType.REGULAR,
+            pltpu.SemaphoreType.REGULAR,
         ],
         compiler_params=pltpu.CompilerParams(
             collective_id=0, has_side_effects=True, vmem_limit_bytes=60 << 20

time: 26.1 us -> 25.8 us (0.989)
  Pallas kernels: 25.3 us -> 25 us
where the time goes in v5:
time: 25.8 us; the launch traced here: 25.7 us
  Pallas kernels  25 us (97%)
  local copies, waits for them, and re-layouts  0.63 us (2%)
    pallas_call x1, Pallas kernels, on_device(): pl.pallas_call(operator_kernel, out_shape=pltpu.VMEM((SUB, features), BF1...  25 us
    unnamed x1, local copies, waits for them, and re-layouts  0.63 us

profile of v5, /device:TPU:480, one launch (start us, length us, event | category | flops | bytes accessed | tf_op | source)
XLA Modules:
  0.0 25.7 jit_solution(15450113489173385279)
XLA Ops:
  0.0 25.0 %shard_map.73 = bf16[8,4096]{1,0:T(8,128)(2,1)S(1)} custom-call(bf16[128,256]{1,0:T(8,128)(2,1)} %q_hbm.1, bf16[128,256]{1,0:T(8,128)(2,1)} %k_hbm.1, bf16[128,256]{1,0:T(8,128)(2,1)} %v_hbm.1, f32[16,256]{1,0:T(8,128)} %bitcast.3, f32[16,256]{1,0:T(8,128)} %bitcast.4, f32[1,256]{1,0:T(1,128)} %bitcast.5, bf16[256,4096]{1,0:T(8,128)(2,1)} %w_hbm.1), custom_call_target="tpu_custom_call" | custom-call | tf_op jit(solution)/shard_map/pallas_call | solution.py:553
  25.0 0.6 %copy.9 = bf16[8,4096]{1,0:T(8,128)(2,1)} copy(bf16[8,4096]{1,0:T(8,128)(2,1)S(1)} %shard_map.73) | data formatting | bytes 131072

commit v6 on v5

--- a/solution.py
+++ b/solution.py
@@ -13,10 +13,11 @@
 
 SIDE = 4
 SUB = 8
-HEAD = (0, 0, 1, 0, 3, 3, 3, 6, 6, 6, 6, 6, 0, 0, 0, 0)
+HEAD = (0, 0, 1, 0, 3, 3, 3, 3, 6, 6, 6, 6, 0, 0, 0, 0)
 HUB, HUB_HEAD, HUB_LAST, HUB_TO = 0, 3, 6, (12, 13, 14, 15)
 PAIR = 8
-LATE = {HUB: HUB_TO, 6: (8, 9, 10, 11)}
+PASS, PASS_TO = 7, (8, 9, 10, 11)
+LATE = {HUB: HUB_TO, PASS: PASS_TO}
 LEVELS = 2
 
 
@@ -109,14 +110,12 @@
         plain[j] += list(range(start, j))
         if j > PAIR:
             whole[j].append(PAIR)
-        if j not in HUB_TO:
+        if j not in HUB_TO and j not in PASS_TO:
             whole[j].append(HEAD[j])
     plain[HUB] += list(range(HUB_HEAD + 1, HUB_LAST + 1))
     whole[HUB].append(HUB_HEAD)
     late = {j: k for k, group in LATE.items() for j in group}
-    greeted = {
-        j: [k for k in plain[j] + whole[j] if late.get(j) != k] for j in range(blocks)
-    }
+    greeted = {j: plain[j] + whole[j] for j in range(blocks)}
     expected = pick(
         [
             sum(i in greeted[j] for j in range(blocks)) + (i in late)
@@ -141,7 +140,7 @@
             ],
         )
 
-    heads = among({k for j in range(blocks) for k in whole[j]} - {PAIR})
+    heads = among({k for j in range(blocks) for k in whole[j]} - {PAIR} | {PASS})
     barrier = pltpu.get_barrier_semaphore()
 
     for source in (*range(PAIR, blocks), *range(PAIR)):
@@ -232,9 +231,9 @@
                 device_id_type=MESH,
             )
 
-    def message(buffer, sems, j):
+    def message(buffer, sems, j, slot=z):
         return remote(
-            buffer, got.at[z], sems.at[j], c_recv.at[z], {"ctx": jnp.int32(j)}
+            buffer, got.at[slot], sems.at[j], c_recv.at[slot], {"ctx": jnp.int32(j)}
         )
 
     def arrived(source):
@@ -299,11 +298,14 @@
 
             @pl.when(z == k)
             def _():
-                targets = [j for j in range(blocks) if k in whole[j]]
-                send_whole(k, [j for j in targets if late.get(j) != k])
-                if k in LATE and k != HUB:
-                    pl.semaphore_wait(ready, len(LATE[k]))
-                    send_whole(k, [j for j in targets if late.get(j) == k])
+                send_whole(k, [j for j in range(blocks) if k in whole[j]])
+
+        @pl.when(z == PASS)
+        def _():
+            pre_msg[...] = carry[...].astype(BF16)
+            pl.semaphore_wait(ready, len(PASS_TO))
+            for j in reversed(PASS_TO):
+                message(pre_msg, p_send, j, jnp.int32(HUB_LAST)).start()
 
     def hub_step():
         @pl.when(z == HUB)
@@ -519,7 +521,7 @@
             def _():
                 message(own_msg, e_send, j).wait_send()
 
-        senders = whole[j] + ([HUB] if j in HUB_TO else [])
+        senders = whole[j] + [k for k in LATE if j in LATE[k]]
         if senders:
 
             @pl.when(among(senders))

time: 25.8 us -> 25.8 us (level)
  no operation moved by 1% of the time
where the time goes in v6:
time: 25.8 us; the launch traced here: 25.7 us
  Pallas kernels  25 us (97%)
  local copies, waits for them, and re-layouts  0.63 us (2%)
    pallas_call x1, Pallas kernels, on_device(): pl.pallas_call(operator_kernel, out_shape=pltpu.VMEM((SUB, features), BF1...  25 us
    unnamed x1, local copies, waits for them, and re-layouts  0.63 us

profile of v6, /device:TPU:480, one launch (start us, length us, event | category | flops | bytes accessed | tf_op | source)
XLA Modules:
  0.0 25.7 jit_solution(15148573680199169741)
XLA Ops:
  0.0 25.0 %shard_map.73 = bf16[8,4096]{1,0:T(8,128)(2,1)S(1)} custom-call(bf16[128,256]{1,0:T(8,128)(2,1)} %q_hbm.1, bf16[128,256]{1,0:T(8,128)(2,1)} %k_hbm.1, bf16[128,256]{1,0:T(8,128)(2,1)} %v_hbm.1, f32[16,256]{1,0:T(8,128)} %bitcast.3, f32[16,256]{1,0:T(8,128)} %bitcast.4, f32[1,256]{1,0:T(1,128)} %bitcast.5, bf16[256,4096]{1,0:T(8,128)(2,1)} %w_hbm.1), custom_call_target="tpu_custom_call" | custom-call | tf_op jit(solution)/shard_map/pallas_call | solution.py:555
  25.0 0.6 %copy.9 = bf16[8,4096]{1,0:T(8,128)(2,1)} copy(bf16[8,4096]{1,0:T(8,128)(2,1)S(1)} %shard_map.73) | data formatting | bytes 131072

commit v7 on v6

--- a/solution.py
+++ b/solution.py
@@ -253,7 +253,7 @@
         ).astype(BF16)
         send_whole(PAIR, [j for j in range(blocks) if PAIR in whole[j]])
 
-    for j in reversed(range(blocks)):
+    for j in (0, *reversed(range(1, blocks))):
         if plain[j]:
 
             @pl.when(among(plain[j]))
@@ -280,15 +280,17 @@
 
             carry[...] = carry[...] * decay_block + got[source].astype(F32)
 
+        @pl.when(jnp.logical_and(z > 0, z <= PAIR))
+        def _():
+            arrived(head)
+            carry[...] += head_decay * got[head].astype(F32)
+
         @pl.when(z > PAIR)
         def _():
             arrived(jnp.int32(PAIR))
-            carry[...] += pair_decay * got[PAIR].astype(F32)
-
-        @pl.when(z > 0)
-        def _():
+            known = carry[...] + pair_decay * got[PAIR].astype(F32)
             arrived(head)
-            carry[...] += head_decay * got[head].astype(F32)
+            carry[...] = known + head_decay * got[head].astype(F32)
 
     @pl.when(heads)
     def _():
@@ -317,7 +319,7 @@
                 total = block if total is None else total * decay_block + block
             hub_msg[...] = total.astype(BF16)
             pl.semaphore_wait(ready, len(HUB_TO))
-            for j in reversed(HUB_TO):
+            for j in HUB_TO:
                 message(hub_msg, p_send, j).start()
 
     for half in range(2):

time: 25.8 us -> 25.8 us (level)
  no operation moved by 1% of the time
where the time goes in v7:
time: 25.8 us; the launch traced here: 25.7 us
  Pallas kernels  25 us (97%)
  local copies, waits for them, and re-layouts  0.63 us (2%)
    pallas_call x1, Pallas kernels, on_device(): pl.pallas_call(operator_kernel, out_shape=pltpu.VMEM((SUB, features), BF1...  25 us
    unnamed x1, local copies, waits for them, and re-layouts  0.63 us

profile of v7, /device:TPU:480, one launch (start us, length us, event | category | flops | bytes accessed | tf_op | source)
XLA Modules:
  0.0 25.7 jit_solution(4701034418602466370)
XLA Ops:
  0.0 25.0 %shard_map.73 = bf16[8,4096]{1,0:T(8,128)(2,1)S(1)} custom-call(bf16[128,256]{1,0:T(8,128)(2,1)} %q_hbm.1, bf16[128,256]{1,0:T(8,128)(2,1)} %k_hbm.1, bf16[128,256]{1,0:T(8,128)(2,1)} %v_hbm.1, f32[16,256]{1,0:T(8,128)} %bitcast.3, f32[16,256]{1,0:T(8,128)} %bitcast.4, f32[1,256]{1,0:T(1,128)} %bitcast.5, bf16[256,4096]{1,0:T(8,128)(2,1)} %w_hbm.1), custom_call_target="tpu_custom_call" | custom-call | tf_op jit(solution)/shard_map/pallas_call | solution.py:557
  25.0 0.6 %copy.9 = bf16[8,4096]{1,0:T(8,128)(2,1)} copy(bf16[8,4096]{1,0:T(8,128)(2,1)S(1)} %shard_map.73) | data formatting | bytes 131072

commit v8 on v7

--- a/solution.py
+++ b/solution.py
@@ -219,6 +219,27 @@
     own_msg[...] = state[...].astype(BF16)
     decay_block = jnp.exp(-float(tokens) * dec[...])
 
+    def message(buffer, sems, j, slot=z):
+        return remote(
+            buffer, got.at[slot], sems.at[j], c_recv.at[slot], {"ctx": jnp.int32(j)}
+        )
+
+    def arrived(source):
+        remote(
+            own_msg, got.at[source], e_send.at[0], c_recv.at[source], {"ctx": z}
+        ).wait_recv()
+
+    def send_whole(k, targets):
+        for j in reversed(targets):
+            message(pre_msg, p_send, j).start()
+
+    @pl.when(z == PAIR)
+    def _():
+        arrived(jnp.int32(PAIR - 1))
+        pre_msg[...] = (
+            state[...] + decay_block * got[PAIR - 1].astype(F32)
+        ).astype(BF16)
+
     pl.semaphore_wait(barrier, 2 * (SIDE - 1) + expected + 1 - core)
     for source, group in LATE.items():
 
@@ -231,26 +252,8 @@
                 device_id_type=MESH,
             )
 
-    def message(buffer, sems, j, slot=z):
-        return remote(
-            buffer, got.at[slot], sems.at[j], c_recv.at[slot], {"ctx": jnp.int32(j)}
-        )
-
-    def arrived(source):
-        remote(
-            own_msg, got.at[source], e_send.at[0], c_recv.at[source], {"ctx": z}
-        ).wait_recv()
-
-    def send_whole(k, targets):
-        for j in reversed(targets):
-            message(pre_msg, p_send, j).start()
-
     @pl.when(z == PAIR)
     def _():
-        arrived(jnp.int32(PAIR - 1))
-        pre_msg[...] = (
-            state[...] + decay_block * got[PAIR - 1].astype(F32)
-        ).astype(BF16)
         send_whole(PAIR, [j for j in range(blocks) if PAIR in whole[j]])
 
     for j in (0, *reversed(range(1, blocks))):

time: 25.8 us -> 25.8 us (level)
  no operation moved by 1% of the time
where the time goes in v8:
time: 25.8 us; the launch traced here: 25.7 us
  Pallas kernels  25 us (97%)
  local copies, waits for them, and re-layouts  0.63 us (2%)
    pallas_call x1, Pallas kernels, on_device(): pl.pallas_call(operator_kernel, out_shape=pltpu.VMEM((SUB, features), BF1...  25 us
    unnamed x1, local copies, waits for them, and re-layouts  0.63 us

profile of v8, /device:TPU:480, one launch (start us, length us, event | category | flops | bytes accessed | tf_op | source)
XLA Modules:
  0.0 25.7 jit_solution(9670723577362199847)
XLA Ops:
  0.0 25.0 %shard_map.73 = bf16[8,4096]{1,0:T(8,128)(2,1)S(1)} custom-call(bf16[128,256]{1,0:T(8,128)(2,1)} %q_hbm.1, bf16[128,256]{1,0:T(8,128)(2,1)} %k_hbm.1, bf16[128,256]{1,0:T(8,128)(2,1)} %v_hbm.1, f32[16,256]{1,0:T(8,128)} %bitcast.3, f32[16,256]{1,0:T(8,128)} %bitcast.4, f32[1,256]{1,0:T(1,128)} %bitcast.5, bf16[256,4096]{1,0:T(8,128)(2,1)} %w_hbm.1), custom_call_target="tpu_custom_call" | custom-call | tf_op jit(solution)/shard_map/pallas_call | solution.py:560
  25.0 0.6 %copy.9 = bf16[8,4096]{1,0:T(8,128)(2,1)} copy(bf16[8,4096]{1,0:T(8,128)(2,1)S(1)} %shard_map.73) | data formatting | bytes 131072
